TPU v7x, 32 devices: a whole 2x2x4 slice. The times are simulated.
32 devices in a mesh: dp: 16 (over z, x, core), tensor: 2 (over y).
Axes of the slice: x: 2, y: 2, z: 4, core: 2. Of those that a mesh axis runs over, the one named last changes fastest.
Arguments:
- inputs: bfloat16 [32768, 512], P('dp'), may hold values from -6 to 6
- memory: bfloat16 [32768, 512], P('dp'), may hold values from -6 to 6
- tgt_seg: int32 [32, 1024], P('dp'), may hold values from 0 to 31, as said below
- src_seg: int32 [32, 1024], P('dp'), may hold values from 0 to 31, as said below
- self_query: bfloat16 [512, 512], P(None, 'tensor'), may hold values from -0.25 to 0.25
- self_key: bfloat16 [512, 512], P(None, 'tensor'), may hold values from -0.25 to 0.25
- self_value: bfloat16 [512, 512], P(None, 'tensor'), may hold values from -0.25 to 0.25
- self_out: bfloat16 [512, 512], P('tensor'), may hold values from -1 to 1
- cross_query: bfloat16 [512, 512], P(None, 'tensor'), may hold values from -0.25 to 0.25
- cross_key: bfloat16 [512, 512], P(None, 'tensor'), may hold values from -0.25 to 0.25
- cross_value: bfloat16 [512, 512], P(None, 'tensor'), may hold values from -0.25 to 0.25
- cross_out: bfloat16 [512, 512], P('tensor'), may hold values from -1 to 1
- ffn_in: bfloat16 [512, 2048], P(None, 'tensor'), may hold values from -0.25 to 0.25
- ffn_out: bfloat16 [2048, 512], P('tensor'), may hold values from -0.125 to 0.125
- norm_gain: float32 [3, 512], replicated, may hold values from 0.25 to 1.75
- norm_shift: float32 [3, 512], replicated, may hold values from -3 to 3
- residual_scale: float32 [3, 512], replicated, may hold values from 0.8 to 2
- cotangent: bfloat16 [32768, 512], P('dp')
Outputs:
- output: bfloat16 [32768, 512], P('dp')
- input_grad: float32 [32768, 512], P('dp', 'tensor')
- memory_grad: float32 [32768, 512], P('dp', 'tensor')
- self_query_grad: float32 [512, 512], P('dp', 'tensor')
- self_key_grad: float32 [512, 512], P('dp', 'tensor')
- self_value_grad: float32 [512, 512], P('dp', 'tensor')
- self_out_grad: float32 [512, 512], P('tensor', 'dp')
- cross_query_grad: float32 [512, 512], P('dp', 'tensor')
- cross_key_grad: float32 [512, 512], P('dp', 'tensor')
- cross_value_grad: float32 [512, 512], P('dp', 'tensor')
- cross_out_grad: float32 [512, 512], P('tensor', 'dp')
- ffn_in_grad: float32 [512, 2048], P('dp', 'tensor')
- ffn_out_grad: float32 [2048, 512], P('tensor', 'dp')
- norm_gain_grad: float32 [3, 512], P(None, 'dp')
- norm_shift_grad: float32 [3, 512], P(None, 'dp')
- residual_scale_grad: float32 [3, 512], P(None, 'dp')
Inputs may be any that keep to these rules, and one draw needn't show every extreme that they name: `tgt_seg`: along each row the ids never fall, and every id from 0 to 31 holds one or more positions of every row; target id s of row r is the same sentence pair as memory id s of row r. `src_seg`: along each row the ids never fall, and every id from 0 to 31 holds one or more positions of every row.
All inputs are finite; a program needn't handle non-finite values.
Results may differ from a plain program's by a relative error of at most 0.025.
Values may be sent and summed in bfloat16 or wider, within the bound.
No kernel may reach another device: no remote copies, remote signals or barrier semaphores. Data moves between devices by JAX's collectives and lax.ppermute only.
A program may use at most 192 MiB of HBM per device.

v0:
```python
import functools
import math

import jax
import jax.numpy as jnp
from jax import lax
from jax.experimental import pallas as pl
from jax.experimental.pallas import tpu as pltpu
from jax.sharding import PartitionSpec as P

HEAD_DIM = 64
QB = 128
KC = 256
XC = 128
GW = 256
EPS = 1e-05
NEG = -1e30
F32 = jnp.float32
BF16 = jnp.bfloat16
MB = 512
SPARE = 12 * 1024 * 1024
FULL = 56 * 1024 * 1024
SEGMENTS = 32
FLOPS_PER_US = 5e9


def nn(left, right):
    return lax.dot_general(left, right, (((1,), (0,)), ((), ())), preferred_element_type=F32)


def nt(left, right):
    return lax.dot_general(left, right, (((1,), (1,)), ((), ())), preferred_element_type=F32)


def tn(left, right):
    return lax.dot_general(left, right, (((0,), (0,)), ((), ())), preferred_element_type=F32)


def iota(shape, dim):
    return lax.broadcasted_iota(jnp.int32, shape, dim)


def normalise(pre):
    center = jnp.mean(pre, axis=-1, keepdims=True)
    centered = pre - center
    rstd = lax.rsqrt(jnp.mean(centered * centered, axis=-1, keepdims=True) + EPS)
    return centered * rstd, rstd


def norm_back(grad, gain, xhat, rstd):
    scaled = grad * gain
    first = jnp.mean(scaled, axis=-1, keepdims=True)
    second = jnp.mean(scaled * xhat, axis=-1, keepdims=True)
    return rstd * (scaled - first - xhat * second)


def rows_at(block, size):
    return pl.ds(pl.multiple_of(block * size, size), size)


def stack_heads(block):
    head = iota((1, GW), 1) // HEAD_DIM
    return jnp.concatenate(
        [block * (head == h).astype(F32).astype(BF16) for h in range(GW // HEAD_DIM)], axis=0
    )


def unstack_heads(stacked, rows):
    low_half = iota((1, 128), 1) < HEAD_DIM
    tiles = []
    for tile in range(GW // 128):
        cols = slice(tile * 128, tile * 128 + 128)
        first, second = 2 * tile, 2 * tile + 1
        tiles.append(
            jnp.where(
                low_half,
                stacked[first * rows : (first + 1) * rows, cols],
                stacked[second * rows : (second + 1) * rows, cols],
            )
        )
    return jnp.concatenate(tiles, axis=1)


def each_more(units, where, body):
    if all(unit[where] is units[0][where] for unit in units):

        @pl.loop(1, units[0][where])
        def _(j):
            for n in range(len(units)):
                body(n, j)

    else:
        for n, unit in enumerate(units):

            @pl.loop(1, unit[where])
            def _(j):
                body(n, j)


def chunk_keys(first, j):
    if isinstance(j, int):
        return pl.ds(pl.multiple_of(first, 16), KC)
    return pl.ds(pl.multiple_of(first + (KC - XC) + j * XC, 16), XC)


def attend_units(units, s_scr, m_scr, l_scr, o_scr):
    heads = GW // HEAD_DIM
    stacks = [stack_heads(q[rows_at(i, QB), :]) for i, q, *_ in units]

    def scores(n, j):
        _, _, k, _, lo, hi, first, _ = units[n]
        keys, place = chunk_keys(first, j), chunk_keys(0, j)
        at = keys.start + iota((keys.size, QB), 0)
        allowed = (at >= lo) & (at < hi)
        s = nt(k[keys, :], stacks[n])
        peaks = []
        for h in range(heads):
            part = slice(h * QB, (h + 1) * QB)
            masked = jnp.where(allowed, s[:, part], NEG)
            s_scr[n, place, part] = masked
            peaks.append(jnp.max(masked, axis=0, keepdims=True))
        return jnp.concatenate(peaks, axis=1)

    for n in range(len(units)):
        m_scr[n : n + 1, :] = scores(n, 0)

    def more_scores(n, j):
        m_scr[n : n + 1, :] = jnp.maximum(m_scr[n : n + 1, :], scores(n, j))

    each_more(units, 7, more_scores)
    peaks = [m_scr[n : n + 1, :] for n in range(len(units))]

    def weigh(n, j):
        p = jnp.exp(s_scr[n, chunk_keys(0, j), :] - peaks[n])
        return jnp.sum(p, axis=0, keepdims=True), tn(units[n][3][chunk_keys(units[n][6], j), :], p.astype(BF16))

    for n in range(len(units)):
        l_scr[n : n + 1, :], o_scr[n] = weigh(n, 0)

    def more_weights(n, j):
        more_l, more_o = weigh(n, j)
        l_scr[n : n + 1, :] = l_scr[n : n + 1, :] + more_l
        o_scr[n] = o_scr[n] + more_o

    each_more(units, 7, more_weights)
    results = []
    for n in range(len(units)):
        total = l_scr[n : n + 1, :]
        log = peaks[n] + jnp.log(total)
        scale = 1.0 / total
        parts = [
            o_scr[n, h * HEAD_DIM : (h + 1) * HEAD_DIM, h * QB : (h + 1) * QB] * scale[:, h * QB : (h + 1) * QB]
            for h in range(heads)
        ]
        mixed = jnp.transpose(jnp.concatenate(parts, axis=0).astype(BF16))
        results.append((mixed, [log[:, h * QB : (h + 1) * QB] for h in range(heads)]))
    return results


def attend_back_units(units, r_scr):
    heads = GW // HEAD_DIM

    def chunk(n, j):
        i, q, k, v, do, lse, delta, lo, hi, first, _, _, dk, dv = units[n]
        rows = rows_at(i, QB)
        keys = chunk_keys(first, j)
        qs = stack_heads(q[rows, :])
        ds = stack_heads(do[rows, :])
        kg = k[keys, :]
        at = keys.start + iota((keys.size, QB), 0)
        allowed = (at >= lo) & (at < hi)
        st = nt(kg, qs)
        dp = nt(v[keys, :], ds)
        probs, grads = [], []
        for h in range(heads):
            part = slice(h * QB, (h + 1) * QB)
            p = jnp.where(allowed, jnp.exp(st[:, part] - lse[h : h + 1, rows]), 0.0)
            probs.append(p.astype(BF16))
            grads.append((p * (dp[:, part] - delta[h : h + 1, rows])).astype(BF16))
        prob = jnp.concatenate(probs, axis=1)
        grad = jnp.concatenate(grads, axis=1)
        dv[keys, :] += nn(prob, ds)
        dk[keys, :] += nn(grad, qs)
        return tn(grad, kg)

    for n in range(len(units)):
        r_scr[n] = chunk(n, 0)

    def more(n, j):
        r_scr[n] = r_scr[n] + chunk(n, j)

    each_more(units, 10, more)
    for n, unit in enumerate(units):
        unit[11][rows_at(unit[0], QB), :] = (unstack_heads(r_scr[n], QB) * HEAD_DIM**-0.5).astype(BF16)


def set_delta(rows, do, mixed, delta_scr):
    heads = do.shape[1] // HEAD_DIM
    product = do.astype(F32) * mixed.astype(F32)
    high = product.astype(BF16)
    rest = (product - high.astype(F32)).astype(BF16)
    pick = (iota((heads, do.shape[1]), 1) // HEAD_DIM == iota((heads, do.shape[1]), 0)).astype(F32).astype(BF16)
    delta_scr[:, rows] = nt(pick, high) + nt(pick, rest)


def put_transposed(rows, block, scr, chunk):
    turned = jnp.transpose(block)
    size = turned.shape[0]
    count = size // chunk
    for n in range(count):
        first = (n % 2 * 2 + n // 2 % 2) * (size // 4) + n // 4 * chunk if chunk else 0
        scr[first : first + chunk, rows] = turned[n * chunk : (n + 1) * chunk]


def add_sum(ref, row, value):
    ref[row : row + 1, :] += jnp.sum(value, axis=0, keepdims=True)


def project(rows, left, weight, out, factor=1.0):
    out[rows, :] = (nn(left, weight[...]) * factor).astype(BF16)


def unpack_square(mine, sib, weights):
    core = core_index()
    *cols, out = weights
    part, half = cols[0].shape[0] // 2, out.shape[0]
    small = half // 2
    for place, source in ((core, mine), (1 - core, sib)):
        for n, w in enumerate(cols):
            w[rows_at(place, part), :] = source[n * part : (n + 1) * part, :]
        base = len(cols) * part
        for n in range(out.shape[1] // half):
            out[rows_at(place, small), n * half : (n + 1) * half] = source[
                base + n * small : base + (n + 1) * small, :
            ]


def unpack_ffn(mine, sib, win, wout):
    core = core_index()
    part, rows, width = win.shape[0] // 2, wout.shape[0] // 2, wout.shape[1]
    tiles = win.shape[1] // width
    for place, source in ((core, mine), (1 - core, sib)):
        for n in range(tiles):
            win[rows_at(place, part), n * width : (n + 1) * width] = source[n * part : (n + 1) * part, :]
        wout[rows_at(place, rows), :] = source[tiles * part :, :]


def core_index():
    return lax.axis_index("dp") % 2


def set_ranges(tgt, src, brow, blocks):
    rows, length = tgt.shape
    mine = lax.axis_index("tensor")

    def row(ref):
        value = ref[0:1, :]
        for n in range(1, rows):
            value = jnp.where(mine == n, ref[n : n + 1, :], value)
        return value

    target, source = row(tgt), row(src)
    ids = iota((SEGMENTS, length), 0)

    def before(ids_of, limit):
        count = jnp.sum((ids_of < limit).astype(F32), axis=1, keepdims=True)
        return jnp.sum(jnp.where(ids == target, count, 0.0), axis=0, keepdims=True).astype(jnp.int32)

    values = [
        before(target, ids), iota((1, length), 1) + 1, before(source, ids), before(source, ids + 1)
    ]
    lane = iota((1, 128), 1)
    for n, value in enumerate(values):
        brow[n : n + 1, :] = value
        brow[n + 4 : n + 5, :] = value
    blocks[...] = jnp.zeros_like(blocks)
    for n in range(2):
        first = jnp.zeros((1, 128), jnp.int32)
        last = jnp.zeros((1, 128), jnp.int32)
        for i in range(length // QB):
            low, high = values[2 * n][:, i * QB : i * QB + 1], values[2 * n + 1][:, (i + 1) * QB - 1 : (i + 1) * QB]
            first = jnp.where(lane == i, low, first)
            last = jnp.where(lane == i, high, last)
        first = lax.shift_left(lax.shift_right_logical(first, 4), 4)
        more = lax.shift_right_logical(jnp.maximum(last - first - KC, 0) + (XC - 1), XC.bit_length() - 1)
        blocks[2 * n : 2 * n + 1, :] = jnp.minimum(first, length - KC - more * XC)
        blocks[2 * n + 1 : 2 * n + 2, :] = more + 1


def forward_units(sc, brow, i, which, groups):
    rows = rows_at(i, QB)
    first, count = sc[2 * which, i], sc[2 * which + 1, i]
    lo, hi = brow[2 * which : 2 * which + 1, rows], brow[2 * which + 1 : 2 * which + 2, rows]
    return [(i, q, k, v, lo, hi, first, count) for q, k, v in groups]


def put_logs(lse, i, logs):
    for h, log in enumerate(logs):
        lse[h : h + 1, rows_at(i, QB)] = log


def project_self(x, weights, outs):
    @pl.loop(0, x.chunks)
    def _(i):
        x.need(i)
        rows = rows_at(i, MB)
        block = x[rows, :]
        for weight, out, factor in zip(weights, outs, (HEAD_DIM**-0.5, 1.0, 1.0)):
            project(rows, block, weight, out, factor)
            out.put(i)


def self_forward_own(sc, qo, ko, vo, x, brow, q, k, v, mixed, lse, *scratch):
    need(qo, ko, vo)
    project_self(x, (qo, ko, vo), (q, k, v))
    need(brow)

    @pl.loop(0, x.shape[0] // QB // 2)
    def _(pair):
        pair_of = [2 * pair, 2 * pair + 1]
        units = [forward_units(sc, brow, i, 0, [(q, k, v)])[0] for i in pair_of]
        for i, (block, logs) in zip(pair_of, attend_units(units, *scratch)):
            mixed[rows_at(i, QB), :] = block
            put_logs(lse, i, logs)


def norm_rows(i, pre, xhat, rstd):
    @pl.loop(0, MB // QB)
    def _(n):
        rows = rows_at(i * (MB // QB) + n, QB)
        hat, inv = normalise(pre[rows_at(n, QB), :])
        xhat[rows, :] = hat
        rstd[rows, :] = jnp.broadcast_to(inv, (QB, rstd.shape[1]))

    xhat.put(i)
    rstd.put(i)


def self_forward_rest(
    sc, mine, sib, x, brow, mixed_own, oo, omega,
    q, k, v, mixed, lse, xhat, rstd, qx, kx, vx, ox, pre, *scratch,
):
    need(mine, sib)
    unpack_square(mine, sib, (qx, kx, vx, ox))
    project_self(x, (qx, kx, vx), (q, k, v))
    need(brow)

    @pl.loop(0, x.shape[0] // QB // 2)
    def _(pair):
        pair_of = [2 * pair, 2 * pair + 1]
        units = [forward_units(sc, brow, i, 0, [(q, k, v)])[0] for i in pair_of]
        for i, (block, logs) in zip(pair_of, attend_units(units, *scratch)):
            mixed[rows_at(i, QB), :] = block
            put_logs(lse, i, logs)

    need(mixed_own, oo, omega)

    @pl.loop(0, x.chunks)
    def _(i):
        rows = rows_at(i, MB)
        branch = nn(mixed_own[rows, :], oo[...]) + nn(mixed[rows, :], ox[...])
        pre[...] = omega[0:1] * x[rows, :].astype(F32) + branch
        norm_rows(i, pre, xhat, rstd)


def cross_forward(
    sc, mine, sib, qo, ko, vo, gain, shift, xhat1, mem, brow, oo, omega,
    q, k, v, mixed, lse, q_x, k_x, v_x, mixed_x, lse_x, xhat, rstd, qx, kx, vx, ox, pre, *scratch,
):
    need(mine, sib, qo, ko, vo, gain, shift)
    unpack_square(mine, sib, (qx, kx, vx, ox))

    @pl.loop(0, mem.chunks)
    def _(i):
        rows = rows_at(i, MB)
        xhat1.need(i)
        mem.need(i)
        low1 = (xhat1[rows, :] * gain[0:1] + shift[0:1]).astype(BF16)
        block = mem[rows, :]
        for weights, outs in (((qo, ko, vo), (q, k, v)), ((qx, kx, vx), (q_x, k_x, v_x))):
            project(rows, low1, weights[0], outs[0], HEAD_DIM**-0.5)
            project(rows, block, weights[1], outs[1])
            project(rows, block, weights[2], outs[2])
            for result in outs:
                result.put(i)

    need(brow)

    @pl.loop(0, mem.shape[0] // QB)
    def _(i):
        units = forward_units(sc, brow, i, 1, ((q, k, v), (q_x, k_x, v_x)))
        for (block, logs), out, lse_out in zip(attend_units(units, *scratch), (mixed, mixed_x), (lse, lse_x)):
            out[rows_at(i, QB), :] = block
            put_logs(lse_out, i, logs)

    need(oo, omega)

    @pl.loop(0, mem.chunks)
    def _(i):
        rows = rows_at(i, MB)
        branch = nn(mixed[rows, :], oo[...]) + nn(mixed_x[rows, :], ox[...])
        pre[...] = omega[1:2] * (xhat1[rows, :] * gain[0:1] + shift[0:1]) + branch
        norm_rows(i, pre, xhat, rstd)


def hidden_units(rows, low2, win, act, slope, width=512):
    for first in range(0, win.shape[1], width):
        place = slice(first, first + width)
        u = nn(low2, win[:, place])
        square = u * u
        t = jnp.tanh(u * (0.7978845608028654 + (0.7978845608028654 * 0.044715) * square))
        h = 0.5 + 0.5 * t
        a = u * h
        act[rows, place] = a.astype(BF16)
        steep = 2 * 0.7978845608028654 + (6 * 0.7978845608028654 * 0.044715) * square
        slope[rows, place] = (h + a * (1.0 - h) * steep).astype(BF16)


def ffn_forward_own(sc, io, gain, shift, xhat2, oo, omega, act, slope, pre):
    need(io, gain, shift)

    @pl.loop(0, xhat2.chunks)
    def _(i):
        rows = rows_at(i, MB)
        xhat2.need(i)
        norm2 = xhat2[rows, :] * gain[1:2] + shift[1:2]
        hidden_units(rows, norm2.astype(BF16), io, act, slope)
        act.put(i)
        slope.put(i)

    need(oo, omega)

    @pl.loop(0, xhat2.chunks)
    def _(i):
        rows = rows_at(i, MB)
        norm2 = xhat2[rows, :] * gain[1:2] + shift[1:2]
        pre[rows, :] = omega[2:3] * norm2 + nn(act[rows, :], oo[...])
        pre.put(i)


def ffn_forward_rest(
    sc, mine, sib, gain, shift, xhat2, pre, cot, act_own,
    out, out_all, slope, d_pre3, keep, send, sums, act, ix, ox, grad_t, grads, *, chunk,
):
    need(mine, sib, gain, shift)
    unpack_ffn(mine, sib, ix, ox)
    sums[...] = jnp.zeros_like(sums)
    width = 512
    half = ix.shape[1]

    @pl.loop(0, xhat2.chunks)
    def _(i):
        rows = rows_at(i, MB)
        xhat2.need(i)
        hidden_units(rows, (xhat2[rows, :] * gain[1:2] + shift[1:2]).astype(BF16), ix, act, slope)
        slope.put(i)
        pre.need(i)
        cot.need(i)
        pre[rows, :] += nn(act[rows, :], ox[...])

        @pl.loop(0, MB // QB)
        def _(n):
            small = rows_at(i * (MB // QB) + n, QB)
            hat, inv = normalise(pre[small, :])
            result = (hat * gain[2:3] + shift[2:3]).astype(BF16)
            out[small, :] = result
            out_all[small, :] = result
            grad = cot[small, :].astype(F32)
            d_pre = norm_back(grad, gain[2:3], hat, inv)
            d_pre3[small, :] = d_pre
            put_transposed(small, d_pre.astype(BF16), grad_t, chunk)
            add_sum(sums, 0, grad * hat)
            add_sum(sums, 1, grad)
            add_sum(sums, 2, d_pre * (xhat2[small, :] * gain[1:2] + shift[1:2]))

        for result in (out, out_all, d_pre3):
            result.put(i)

    need(act_own)
    for side, right in enumerate((act_own, act)):
        for first in range(0, half, width):
            grads[:, side * half + first : side * half + first + width] = nn(
                grad_t[...], right[:, first : first + width]
            ).astype(BF16)
    put_grads(grads, keep, send)


def put_grads(scr, keep, send):
    dp = lax.axis_index("dp")
    core, x = (dp % 2, dp // 2 % 2) if keep.dealt else (0, 0)
    size, width = scr.shape[0] // 4, keep.shape[1]
    parts = keep.shape[0] // size
    for out, row in ((keep, core), (send, 1 - core)):
        for n in range(parts):
            side = n * 2 // parts
            first = n % 2 * width if parts == 4 else 0
            place = row * 2 + (x if side == 0 else 1 - x)
            out.copy_part(scr.at[rows_at(place, size), first : first + width], n * size)


def ffn_backward(
    sc, oo, io, gain, shift, omega, d_pre3, slope_own, xhat2, slope_rest, mine, sib, rstd2,
    d_pre2, keep, send, sums, up_scr, norm_t, ix, ox, acc, grads, *, chunk,
):
    need(io, oo, gain, shift, omega, mine, sib)
    unpack_ffn(mine, sib, ix, ox)
    sums[...] = jnp.zeros_like(sums)
    half = io.shape[1]
    width = 512

    @pl.loop(0, xhat2.chunks)
    def _(i):
        rows = rows_at(i, MB)
        for argument in (d_pre3, slope_own, xhat2, slope_rest):
            argument.need(i)
        grad = d_pre3[rows, :]
        low = grad.astype(BF16)
        acc[...] = omega[2:3] * grad
        for side, (win, wout, slope) in enumerate(((io, oo, slope_own), (ix, ox, slope_rest))):
            for first in range(0, half, width):
                place = slice(side * half + first, side * half + first + width)
                up_scr[rows, place] = (
                    slope[rows, first : first + width].astype(F32) * nt(low, wout[first : first + width, :])
                ).astype(BF16)
            acc[...] += nt(up_scr[rows, side * half : (side + 1) * half], win[...])

        rstd2.need(i)

        @pl.loop(0, MB // QB)
        def _(n):
            small = rows_at(i * (MB // QB) + n, QB)
            total = acc[rows_at(n, QB), :]
            hat = xhat2[small, :]
            put_transposed(small, (hat * gain[1:2] + shift[1:2]).astype(BF16), norm_t, chunk)
            d_pre2[small, :] = norm_back(total, gain[1:2], hat, rstd2[small, 0:1])
            add_sum(sums, 0, total * hat)
            add_sum(sums, 1, total)

        d_pre2.put(i)

    for first in range(0, 2 * half, width):
        grads[:, first : first + width] = nn(norm_t[...], up_scr[:, first : first + width]).astype(BF16)
    put_grads(grads, keep, send)


def weight_grads(pairs, grads):
    width = grads.shape[1] // 2
    for n, (left, *rights) in enumerate(pairs):
        for side, right in enumerate(rights):
            half = right.shape[1]
            first = side * width + n * half
            grads[:, first : first + half] = nn(left[...], right[...]).astype(BF16)


def backward_units(sc, brow, i, which, groups):
    rows = rows_at(i, QB)
    first, count = sc[2 * which, i], sc[2 * which + 1, i]
    lo, hi = brow[2 * which : 2 * which + 1, rows], brow[2 * which + 1 : 2 * which + 2, rows]
    return [(i, *group[:6], lo, hi, first, count, *group[6:]) for group in groups]


def attention_grads(low, rows, outs):
    for out, weight, was, total in outs:
        value = nt(low, weight[...]).astype(BF16)
        out[rows, :] = value
        set_delta(rows, value, was[rows, :], total)


def cross_backward(
    sc, mine, sib, oo, gain, shift, omega, d_pre2, xhat1, mem, mixed, mixed_x, q, k, v, q_x, k_x, v_x, lse, lse_x,
    brow, qo, ko, vo, rstd1,
    d_pre1, mem_all, mem_send, keep, send, sums,
    qx, kx, vx, ox, do, do_x, delta, delta_x, dq, dq_x, dk, dk_x, dv, dv_x, dkb, dkb_x, dvb, dvb_x, r_scr,
    grad_t, norm_t, mem_t, acc, grads, *, chunk,
):
    need(mine, sib, oo, gain, shift, omega)
    unpack_square(mine, sib, (qx, kx, vx, ox))
    sums[...] = jnp.zeros_like(sums)
    half = qo.shape[1]
    blocks = mem.shape[0] // QB
    for ref in (dk, dk_x, dv, dv_x):
        ref[...] = jnp.zeros_like(ref)

    @pl.loop(0, mem.chunks)
    def _(i):
        rows = rows_at(i, MB)
        for argument in (d_pre2, xhat1, mem, mixed, mixed_x):
            argument.need(i)
        grad = d_pre2[rows, :]
        low = grad.astype(BF16)
        norm1 = xhat1[rows, :] * gain[0:1] + shift[0:1]
        put_transposed(rows, low, grad_t, chunk)
        put_transposed(rows, norm1.astype(BF16), norm_t, chunk)
        put_transposed(rows, mem[rows, :], mem_t, chunk)
        attention_grads(low, rows, ((do, oo, mixed, delta), (do_x, ox, mixed_x, delta_x)))
        add_sum(sums, 0, grad * norm1)

    need(q, k, v, q_x, k_x, v_x, lse, lse_x, brow)

    @pl.loop(0, blocks)
    def _(i):
        groups = (
            (q, k, v, do, lse, delta, dq, dk, dv), (q_x, k_x, v_x, do_x, lse_x, delta_x, dq_x, dk_x, dv_x)
        )
        attend_back_units(backward_units(sc, brow, i, 1, groups), r_scr)

    need(qo, ko, vo, rstd1)
    tensor = lax.axis_index("tensor")

    @pl.loop(0, mem.chunks)
    def _(i):
        rows = rows_at(i, MB)
        acc[...] = omega[1:2] * d_pre2[rows, :] + nt(dq[rows, :], qo[...]) + nt(dq_x[rows, :], qx[...])
        for low, wide in ((dkb, dk), (dkb_x, dk_x), (dvb, dv), (dvb_x, dv_x)):
            low[rows, :] = wide[rows, :].astype(BF16)

        def part(side):
            which = rows_at(side, half)
            return (
                nt(dkb[rows, :], ko[which, :]) + nt(dkb_x[rows, :], kx[which, :])
                + nt(dvb[rows, :], vo[which, :]) + nt(dvb_x[rows, :], vx[which, :])
            )

        mem_all[rows, :] = part(tensor)
        mem_send[rows, :] = part(1 - tensor).astype(BF16)

        @pl.loop(0, MB // QB)
        def _(n):
            small = rows_at(i * (MB // QB) + n, QB)
            total = acc[rows_at(n, QB), :]
            hat = xhat1[small, :]
            d_pre1[small, :] = norm_back(total, gain[0:1], hat, rstd1[small, 0:1])
            add_sum(sums, 1, total * hat)
            add_sum(sums, 2, total)

        for result in (d_pre1, mem_all, mem_send):
            result.put(i)

    weight_grads(
        ((norm_t, dq, dq_x), (mem_t, dkb, dkb_x), (mem_t, dvb, dvb_x), (grad_t, mixed, mixed_x)), grads
    )
    put_grads(grads, keep, send)


def self_backward(
    sc, mine, sib, oo, d_pre1, x, mixed, mixed_x, q, k, v, q_x, k_x, v_x, lse, lse_x, brow, sums1, sums2, sums3, out_other,
    dq, dq_x, dkb, dkb_x, dvb, dvb_x, keep, send, out_all,
    qx, kx, vx, ox, do, do_x, delta, delta_x, dk, dk_x, dv, dv_x, r_scr, grad_t, in_t, sums, all_sums, sums_t, grads, *, chunk,
):
    need(mine, sib, oo)
    unpack_square(mine, sib, (qx, kx, vx, ox))
    blocks = x.shape[0] // QB
    for ref in (sums, all_sums, dk, dk_x, dv, dv_x):
        ref[...] = jnp.zeros_like(ref)

    @pl.loop(0, x.chunks)
    def _(i):
        rows = rows_at(i, MB)
        for argument in (d_pre1, x, mixed, mixed_x):
            argument.need(i)
        grad = d_pre1[rows, :]
        low = grad.astype(BF16)
        block = x[rows, :]
        put_transposed(rows, low, grad_t, chunk)
        put_transposed(rows, block, in_t, chunk)
        attention_grads(low, rows, ((do, oo, mixed, delta), (do_x, ox, mixed_x, delta_x)))
        add_sum(sums, 0, grad * block.astype(F32))

    need(q, k, v, q_x, k_x, v_x, lse, lse_x, brow, sums1, sums2, sums3, out_other)
    out_all.copy_from(out_other.ref)

    @pl.loop(0, blocks)
    def _(i):
        groups = (
            (q, k, v, do, lse, delta, dq, dk, dv), (q_x, k_x, v_x, do_x, lse_x, delta_x, dq_x, dk_x, dv_x)
        )
        attend_back_units(backward_units(sc, brow, i, 0, groups), r_scr)

    for low, wide in ((dkb, dk), (dkb_x, dk_x), (dvb, dv), (dvb_x, dv_x)):
        low[...] = wide[...].astype(BF16)
    for row, source in enumerate(
        (sums1[1:2, :], sums2[0:1, :], sums3[0:1, :], sums1[2:3, :], sums2[1:2, :], sums3[1:2, :], sums[0:1, :],
         sums1[0:1, :], sums3[2:3, :])
    ):
        all_sums[row : row + 1, :] = source
    put_transposed(pl.ds(0, QB), all_sums[...].astype(BF16), sums_t, chunk)
    weight_grads(((in_t, dq, dq_x), (in_t, dkb, dkb_x), (in_t, dvb, dvb_x), (grad_t, mixed, mixed_x)), grads)
    width = grads.shape[1] // 2
    for side in range(2):
        grads[:, (side + 1) * width - QB : (side + 1) * width] = sums_t[...]
    put_grads(grads, keep, send)


def input_backward(
    sc, mine, sib, qo, ko, vo, omega, d_pre1, dq, dq_x, dk, dk_x, dv, dv_x, mem_other, in_all, in_send, mem_all,
    qx, kx, vx, ox,
):
    need(mine, sib, qo, ko, vo, omega)
    unpack_square(mine, sib, (qx, kx, vx, ox))
    half = qo.shape[1]
    tensor = lax.axis_index("tensor")

    @pl.loop(0, d_pre1.chunks)
    def _(i):
        rows = rows_at(i, MB)
        for argument in (d_pre1, dq, dq_x, dk, dk_x, dv, dv_x):
            argument.need(i)

        def part(side):
            which = rows_at(side, half)
            total = omega[0:1, which] * d_pre1[rows, which]
            for grad, weight in ((dq, qo), (dq_x, qx), (dk, ko), (dk_x, kx), (dv, vo), (dv_x, vx)):
                total = total + nt(grad[rows, :], weight[which, :])
            return total

        in_all[rows, :] = part(tensor)
        in_send[rows, :] = part(1 - tensor).astype(BF16)
        in_all.put(i)
        in_send.put(i)

    need(mem_other)
    mem_all[...] = mem_other[...].astype(F32)


def fill_kernel(sc, other, out):
    @pl.loop(0, other.chunks)
    def _(i):
        other.need(i)
        rows = rows_at(i, other.shape[0] // other.chunks)
        out[rows, :] = other[rows, :].astype(out.dtype)
        out.put(i)


def finish(
    sc, own_f, own_c, late, s0, s1, s2, s3, sq, sk, sv, so, cq, ck, cv, co, win, wout, gain, shift, omega
):
    need(own_f, own_c, late, s0, s1, s2, s3)
    half, hidden = sq.shape[1], win.shape[1]

    def late_sum(own, first, base, width):
        return own[:, first : first + width].astype(F32) + late[:, base + first : base + first + width].astype(F32)

    wout[...] = late_sum(own_f, 0, 0, hidden)
    win[...] = late_sum(own_f, hidden, 0, hidden)
    for n, out in enumerate((cq, ck, cv, co)):
        out[...] = late_sum(own_c, n * half, 2 * hidden, half)

    def soon_sum(first, width):
        cols = slice(first, first + width)
        return (s0[:, cols].astype(F32) + s1[:, cols].astype(F32)) + (s2[:, cols].astype(F32) + s3[:, cols].astype(F32))

    for n, out in enumerate((sq, sk, sv, so)):
        out[...] = soon_sum(n * half, half)
    sums = jnp.transpose(soon_sum(4 * half, QB))
    for n, out in enumerate((gain, shift, omega)):
        out[...] = sums[3 * n : 3 * n + 3]


class Buffer:
    def __init__(self, ref, far, sems, chunks):
        self.ref, self.far, self.sems, self.chunks = ref, far, sems, chunks
        self.shape, self.dtype = far.shape, far.dtype

    def __getitem__(self, index):
        return self.ref[index]

    def __setitem__(self, index, value):
        self.ref[index] = value

    def chunk(self, i):
        size = self.shape[0] // self.chunks
        if self.chunks == 1:
            return self.ref, self.far
        rows = rows_at(i, size)
        return self.ref.at[rows], self.far.at[rows]

    def load(self):
        for i in range(self.chunks):
            near, far = self.chunk(i)
            pltpu.make_async_copy(far, near, self.sems.at[i]).start()

    def need(self, i):
        near, far = self.chunk(i)
        pltpu.make_async_copy(far, near, self.sems.at[i]).wait()

    def put(self, i=0):
        near, far = self.chunk(i)
        pltpu.make_async_copy(near, far, self.sems.at[0]).start()

    def copy_part(self, near, first):
        far = self.far.at[first : first + near.shape[0]]
        pltpu.make_async_copy(near, far, self.sems.at[0]).start()

    def copy_from(self, near):
        pltpu.make_async_copy(near, self.far, self.sems.at[0]).start()

    def done(self):
        pltpu.make_async_copy(self.far, self.far, self.sems.at[0]).wait()


def need(*buffers):
    for buffer in buffers:
        for i in range(buffer.chunks):
            buffer.need(i)


def call(
    body, sc, args, outs, scratch, us, picks=None, puts=None, alias=None, cuts=None, out_cuts=None, bare=(), dealt=True,
    full=False,
):
    picks, puts, cuts, out_cuts = picks or {}, puts or {}, cuts or {}, out_cuts or {}

    def block(ref, pick):
        if pick is None:
            return ref
        rows, other = pick
        place = lax.axis_index("tensor")
        return ref.at[rows_at(1 - place if other else place, rows)]

    def size(shape, pick):
        return shape if pick is None else (pick[0], *shape[1:])

    alias = alias or {}
    loads = [n for n in range(len(args)) if n not in alias]
    buffers = [
        *[(size(args[n].shape, picks.get(n)), args[n].dtype) for n in loads],
        *[(size(shape, puts.get(n)), kind) for n, (shape, kind) in enumerate(outs) if n not in bare],
        *scratch,
    ]
    room = sum(math.prod(shape[:-1]) * max(shape[-1], 128) * jnp.dtype(kind).itemsize for shape, kind in buffers)

    def kernel(sc, *refs):
        refs = list(refs)
        ins = [refs.pop(0) for _ in args]
        far_outs = [refs.pop(0) for _ in outs]
        near_ins = [refs.pop(0) for _ in loads]
        near_outs = [None if n in bare else refs.pop(0) for n in range(len(outs))]
        in_sems = [refs.pop(0) for _ in loads]
        out_sems = [refs.pop(0) for _ in outs]
        arguments = [
            Buffer(near, block(ins[n], picks.get(n)), sems, cuts.get(n, 1))
            for n, near, sems in zip(loads, near_ins, in_sems)
        ]
        results = [
            Buffer(near, block(far, puts.get(n)), sems, out_cuts.get(n, 1))
            for n, (far, near, sems) in enumerate(zip(far_outs, near_outs, out_sems))
        ]
        for result in results:
            result.dealt = dealt
        for argument in arguments:
            argument.load()
        body(sc, *arguments, *results, *refs)
        for n, result in enumerate(results):
            if n not in out_cuts and n not in bare:
                result.put()
        for result in results:
            result.done()

    return pl.pallas_call(
        kernel,
        out_shape=[jax.ShapeDtypeStruct(shape, kind) for shape, kind in outs],
        grid_spec=pltpu.PrefetchScalarGridSpec(
            num_scalar_prefetch=1,
            grid=(1,),
            in_specs=[pl.BlockSpec(memory_space=pl.ANY)] * len(args),
            out_specs=[pl.BlockSpec(memory_space=pl.ANY)] * len(outs),
            scratch_shapes=[
                *[pltpu.VMEM(shape, kind) for shape, kind in buffers[: len(buffers) - len(scratch)]],
                *[pltpu.SemaphoreType.DMA((cuts.get(n, 1),)) for n in loads],
                *[pltpu.SemaphoreType.DMA((1,)) for _ in outs],
                *[pltpu.VMEM(shape, kind) for shape, kind in scratch],
            ],
        ),
        input_output_aliases={n + 1: out for n, out in alias.items()},
        cost_estimate=pl.CostEstimate(flops=int(us * FLOPS_PER_US), bytes_accessed=1024, transcendentals=0),
        compiler_params=pltpu.CompilerParams(vmem_limit_bytes=FULL if full else room + SPARE),
        name=(body.func if isinstance(body, functools.partial) else body).__name__,
    )(sc, *args)


def pack(weights, outs, moves, segments=None):
    extra = [] if segments is None else list(segments)
    length = extra[0].shape[1] if extra else 0
    ranges = [((8, length), jnp.int32), ((8, 128), jnp.int32)] if extra else []

    def pack_weights(*refs):
        refs = list(refs)
        sources = [refs.pop(0) for _ in weights]
        ids = [refs.pop(0) for _ in extra]
        targets = [refs.pop(0) for _ in outs]
        sem = refs.pop()
        core = core_index()
        copies = []
        for n, (which, rows, first, out, start) in enumerate(moves):
            width = outs[out][0][1]
            copies.append(
                pltpu.make_async_copy(
                    sources[which].at[rows_at(core, rows), first : first + width],
                    targets[out].at[start : start + rows, :],
                    sem.at[n],
                )
            )
        for copy in copies:
            copy.start()
        if ids:
            set_ranges(*ids, *refs)
        for copy in copies:
            copy.wait()

    near = pl.BlockSpec(memory_space=pltpu.VMEM)
    return pl.pallas_call(
        pack_weights,
        out_shape=[jax.ShapeDtypeStruct(shape, kind) for shape, kind in outs + ranges],
        in_specs=[pl.BlockSpec(memory_space=pltpu.HBM)] * len(weights) + [near] * len(extra),
        out_specs=[near] * len(outs + ranges),
        scratch_shapes=[pltpu.SemaphoreType.DMA((len(moves),))],
        cost_estimate=pl.CostEstimate(flops=int(FLOPS_PER_US), bytes_accessed=1024, transcendentals=0),
        compiler_params=pltpu.CompilerParams(vmem_limit_bytes=60 * 1024 * 1024),
        name="pack_weights",
    )(*weights, *extra)


def local(
    inputs, memory, tgt_seg, src_seg, self_query, self_key, self_value, self_out,
    cross_query, cross_key, cross_value, cross_out, ffn_in, ffn_out,
    norm_gain, norm_shift, residual_scale, cotangent, *, n_dp, n_tensor,
):
    d = lax.axis_index("dp")
    t = lax.axis_index("tensor")
    length = tgt_seg.shape[1]
    model = inputs.shape[1]
    half = model // n_tensor
    hidden = ffn_in.shape[1]
    blocks = length // QB
    chunk = model // n_dp
    dealt = chunk % 16 == 0 and n_dp & (n_dp - 1) == 0
    swap_y = [(0, 1), (1, 0)]

    def swap(n_bit):
        return [(i, i ^ n_bit) for i in range(n_dp)]

    def after(value, *others):
        return lax.optimization_barrier((value, others))[0]

    own_s = [self_query, self_key, self_value, self_out]
    own_c = [cross_query, cross_key, cross_value, cross_out]
    own_f = [ffn_in, ffn_out]
    square = ((4 * half, half), BF16)

    def square_moves(base, out):
        part = model // 2
        moves = [(base + n, part, 0, out, n * part) for n in range(3)]
        return moves + [(base + 3, half // 2, n * half, out, 3 * part + n * half // 2) for n in range(n_tensor)]

    (pack_s,) = pack(own_s, [square], square_moves(0, 0))
    tiles = hidden // model
    pack_c, pack_f, brow, sc = pack(
        own_c + own_f, [square, ((tiles * half + hidden // 2, model), BF16)],
        square_moves(0, 0)
        + [(4, model // 2, n * model, 1, n * model // 2) for n in range(tiles)]
        + [(5, hidden // 2, 0, 1, tiles * model // 2)],
        (tgt_seg, src_seg),
    )
    mine_s = lax.ppermute(pack_s, "tensor", swap_y)

    def fill(whole, other):
        (result,) = call(
            fill_kernel, sc, [whole, other], [(whole.shape, whole.dtype)], [], 1, None, {0: (length, True)}, {0: 0},
            cuts={1: 4}, out_cuts={0: 4},
        )
        return result

    def total(*parts):
        result = parts[0].astype(F32)
        for part in parts[1:]:
            result = result + part.astype(F32)
        return result

    size = model // 4

    def part_total(n, *arrays):
        return total(*[array[n * size : (n + 1) * size] for array in arrays]).astype(BF16)

    def z_send(part):
        far = n_dp // 4
        row = d // 4
        part = part.reshape(far, chunk, -1)
        parts = [lax.dynamic_index_in_dim(part, row, 0, keepdims=False)]
        for step in range(1, far):
            perm = [(i, i % 4 + (i // 4 + step) % far * 4) for i in range(n_dp)]
            out = lax.dynamic_index_in_dim(part, (row + step) % far, 0, keepdims=False)
            parts.append(lax.ppermute(out, "dp", perm))
        return parts

    def reduce_any(keep, send):
        grad = lax.psum_scatter(jnp.concatenate([keep, send]).astype(F32), "dp", scatter_dimension=0, tiled=True)
        width = grad.shape[1] // 2
        return grad[:, :width] + lax.ppermute(grad[:, width:], "tensor", swap_y)

    wide, side = (length, model), (length, half)
    heads = GW // HEAD_DIM
    group = [(side, BF16)] * 4 + [((half // HEAD_DIM, length), F32)]
    square_weights = [((model, half), BF16)] * 3 + [((half, model), BF16)]
    stats = [(wide, F32), ((length, 128), F32)]
    attend_scratch = [
        ((2, length, heads * QB), F32),
        ((2, heads * QB), F32),
        ((2, heads * QB), F32),
        ((2, GW, heads * QB), F32),
    ]
    block_wide = ((MB, model), F32)
    cut = length // MB
    norms = [norm_gain, norm_shift, residual_scale]
    s_own = call(
        self_forward_own, sc, [*own_s[:3], inputs, brow], group, attend_scratch, 7, {3: (length, False)},
        cuts={3: cut}, out_cuts={0: cut, 1: cut, 2: cut},
    )
    s_own, mine_s = lax.optimization_barrier((s_own, mine_s))
    sib_s = lax.ppermute(mine_s, "dp", swap(1))
    mine_c = lax.ppermute(after(pack_c, mine_s), "tensor", swap_y)
    s_rest_stats = call(
        self_forward_rest, sc, [mine_s, sib_s, inputs, brow, s_own[3], self_out, residual_scale], group + stats,
        [*square_weights, block_wide, *attend_scratch], 8, {2: (length, False)},
        cuts={2: cut}, out_cuts={n: cut for n in (0, 1, 2, 5, 6)},
    )
    s_rest_stats, mine_c = lax.optimization_barrier((s_rest_stats, mine_c))
    *s_rest, xhat1, rstd1 = s_rest_stats
    sib_c = lax.ppermute(mine_c, "dp", swap(1))
    mine_f = lax.ppermute(after(pack_f, mine_c), "tensor", swap_y)
    c_stats = call(
        cross_forward, sc,
        [mine_c, sib_c, *own_c[:3], norm_gain, norm_shift, xhat1, memory, brow, cross_out, residual_scale],
        group + group + stats,
        [*square_weights, block_wide, *attend_scratch], 14, {8: (length, False)}, cuts={7: cut, 8: cut},
        out_cuts={n: cut for n in (0, 1, 2, 5, 6, 7, 10, 11)},
    )
    *c_state, xhat2, rstd2 = c_stats
    sums_shape = ((8, model), F32)
    low_side, low_wide = ((length, hidden), BF16), ((length, n_tensor * hidden), BF16)
    f_weights = [((model, hidden), BF16), ((hidden, model), BF16)]
    f_own, mine_f = lax.optimization_barrier((
        call(
            ffn_forward_own, sc, [ffn_in, norm_gain, norm_shift, xhat2, ffn_out, residual_scale],
            [low_side, low_side, (wide, F32)], [], 8, cuts={3: cut}, out_cuts={n: cut for n in range(3)},
        ),
        mine_f,
    ))
    act_own, slope_own, pre_own = f_own
    sib_f = lax.ppermute(mine_f, "dp", swap(1))

    def grads(width, parts=2):
        return [((parts * size, 4 * width // parts), BF16)] * 2

    def core_swap(send):
        return lax.ppermute(send, "dp", swap(1)) if dealt else send

    turned = ((model, length), BF16)
    chunk_rows = chunk if dealt else model // 4
    out_row, output, slope_rest, d_pre3, f1_keep, f1_send, sums3 = call(
        functools.partial(ffn_forward_rest, chunk=chunk_rows), sc,
        [mine_f, sib_f, norm_gain, norm_shift, xhat2, pre_own, cotangent, act_own],
        [(wide, BF16), ((n_tensor * length, model), BF16), low_side, (wide, F32), *grads(hidden), sums_shape],
        [low_side, *f_weights, turned, ((model, 2 * hidden), BF16)], 11,
        {6: (length, False)}, {1: (length, False)}, cuts={4: cut, 5: cut, 6: cut}, out_cuts={n: cut for n in range(4)},
        bare=(4, 5), dealt=dealt,
    )
    out_other = lax.ppermute(out_row, "tensor", swap_y)
    f1_other = core_swap(f1_send)
    back, f1_other = lax.optimization_barrier((
        call(
            functools.partial(ffn_backward, chunk=chunk_rows), sc,
            [ffn_out, ffn_in, *norms, d_pre3, slope_own, xhat2, slope_rest, mine_f, sib_f, rstd2],
            [(wide, F32), *grads(hidden), sums_shape],
            [low_wide, turned, *f_weights, block_wide, ((model, 2 * hidden), BF16)], 12,
            cuts={n: cut for n in (5, 6, 7, 8, 11)}, out_cuts={0: cut}, bare=(1, 2), dealt=dealt,
        ),
        f1_other,
    ))
    d_pre2, f2_keep, f2_send, sums2 = back
    f2_other = core_swap(f2_send)
    if dealt:
        f_there = jnp.concatenate([part_total(1, f1_keep, f1_other), part_total(1, f2_keep, f2_other)], axis=1)
        d_pre2 = after(d_pre2, f_there)
        f_x = lax.ppermute(f_there, "dp", swap(2))
    else:
        f_x = sums2
    logs = ((half // HEAD_DIM, length), F32)
    halves = [((n_tensor * length, half), F32), (side, BF16)]
    back, f_x, out_other = lax.optimization_barrier((
        call(
            functools.partial(cross_backward, chunk=chunk_rows), sc,
            [mine_c, sib_c, cross_out, *norms, d_pre2, xhat1, memory, c_state[3], c_state[8],
             *c_state[:3], *c_state[5:8], c_state[4], c_state[9], brow, *own_c[:3], rstd1],
            [(wide, F32), *halves, *grads(4 * half), sums_shape],
            [*square_weights, *[(side, BF16)] * 2, logs, logs, *[(side, BF16)] * 2, *[(side, F32)] * 4,
             *[(side, BF16)] * 4, ((2, heads * QB, GW), F32), turned, turned, turned, block_wide,
             ((model, 8 * half), BF16)],
            23, {8: (length, False)}, {1: (length, False)}, cuts={n: cut for n in range(6, 11)},
            out_cuts={n: cut for n in range(3)}, bare=(3, 4), dealt=dealt,
        ),
        f_x, out_other,
    ))
    d_pre1, memory_grad, mem_send, c_keep, c_send, sums1 = back
    mem_other = lax.ppermute(mem_send, "tensor", swap_y)
    c_other = core_swap(c_send)
    c_x, f_z = sums1, sums1
    if dealt:
        f_part = jnp.concatenate(
            [
                part_total(
                    0, keep[:, first : first + hidden], other[:, first : first + hidden],
                    f_x[:, base + first : base + first + hidden],
                )
                for first in (0, hidden)
                for keep, other, base in ((f1_keep, f1_other, 0), (f2_keep, f2_other, 2 * hidden))
            ],
            axis=1,
        )
        f_z = z_send(f_part)
        c_there = part_total(1, c_keep, c_other)
        c_x = lax.ppermute(c_there, "dp", swap(2))
        d_pre1 = after(d_pre1, c_there, f_part)
    back, c_x, mem_other = lax.optimization_barrier((
        call(
            functools.partial(self_backward, chunk=chunk_rows), sc,
            [mine_s, sib_s, self_out, d_pre1, inputs, s_own[3], s_rest[3], *s_own[:3],
             *s_rest[:3], s_own[4], s_rest[4], brow, sums1, sums2, sums3, out_other, output],
            [*[(side, BF16)] * 6, *grads(4 * half + QB, 4 if dealt else 2), (output.shape, BF16)],
            [*square_weights, *[(side, BF16)] * 2, logs, logs, *[(side, F32)] * 4,
             ((2, heads * QB, GW), F32), turned, turned, ((8, model), F32), ((QB, model), F32), ((model, QB), BF16),
             ((model, 2 * (4 * half + QB)), BF16)],
            16, {4: (length, False)}, {8: (length, True)}, {20: 8}, cuts={n: cut for n in range(3, 7)},
            bare=(6, 7, 8), dealt=dealt,
        ),
        c_x, mem_other,
    ))
    *d_self, s_keep, s_send, output = back
    s_other = core_swap(s_send)
    if dealt:
        across = [(i * 2 + j, (i ^ 2) * 2 + 1 - j) for i in range(n_dp) for j in range(2)]
        s_near = [part_total(n, s_keep, s_other) for n in range(1, 4)]
        f_last = total(*f_z).astype(BF16)
        c_part = part_total(0, c_keep, c_other, c_x)
        d_self[0] = after(d_self[0], *s_near, f_last, c_part)
        s_near = [
            lax.ppermute(s_near[0], "tensor", swap_y), lax.ppermute(s_near[1], "dp", swap(2)),
            lax.ppermute(s_near[2], ("dp", "tensor"), across),
        ]
        c_z = z_send(c_part)
    input_grad, in_send, memory_grad = call(
        input_backward, sc,
        [mine_s, sib_s, *own_s[:3], residual_scale, d_pre1, *d_self, mem_other, memory_grad],
        [*halves, (memory_grad.shape, F32)], square_weights, 5, None, {0: (length, False), 2: (length, True)},
        {14: 2}, cuts={n: cut for n in range(6, 13)}, out_cuts={0: cut, 1: cut},
    )
    thin, broad = ((chunk, half), F32), ((chunk, hidden), F32)
    three = ((3, chunk), F32)
    if dealt:
        in_send, s_near, c_z = lax.optimization_barrier((in_send, s_near, c_z))
        in_other = lax.ppermute(in_send, "tensor", swap_y)
        s_far = z_send(part_total(0, s_keep, s_other, *s_near))
        c_last = total(*c_z).astype(BF16)
        late = lax.ppermute(
            jnp.concatenate([f_last[:, 2 * hidden :], c_last[:, 4 * half :]], axis=1), "tensor", swap_y
        )
        while len(s_far) < 4:
            s_far.append(jnp.zeros_like(s_far[0]))
        s_far = [*s_far[:3], s_far[3] if len(s_far) == 4 else total(*s_far[3:]).astype(BF16)]
        input_grad = fill(input_grad, in_other)
        sq, sk, sv, so, cq, ck, cv, co, ffn_in_grad, ffn_out_grad, gain_grad, shift_grad, scale_grad = call(
            finish, sc, [f_last, c_last, late, *s_far], [*[thin] * 8, broad, broad, three, three, three], [], 0.01
        )
    else:
        input_grad = fill(input_grad, lax.ppermute(in_send, "tensor", swap_y))
        f1_sum, f2_sum = reduce_any(f1_keep, f1_send), reduce_any(f2_keep, f2_send)
        c_sum, s_sum = reduce_any(c_keep, c_send), reduce_any(s_keep, s_send)
        ffn_in_grad, ffn_out_grad = f2_sum, f1_sum
        cq, ck, cv, co = [c_sum[:, n * half : (n + 1) * half] for n in range(4)]
        sq, sk, sv, so = [s_sum[:, n * half : (n + 1) * half] for n in range(4)]
        gain_grad, shift_grad, scale_grad = [s_sum[:, 4 * half + 3 * n : 4 * half + 3 * n + 3].T for n in range(3)]
    return (
        output, input_grad, memory_grad, sq, sk, sv, so.T, cq, ck, cv, co.T, ffn_in_grad, ffn_out_grad.T,
        gain_grad, shift_grad, scale_grad,
    )


def solution(mesh):
    rows, cols = P("dp", None), P(None, "tensor")
    both, turned = P("dp", "tensor"), P("tensor", "dp")
    return jax.shard_map(
        functools.partial(local, n_dp=mesh.shape["dp"], n_tensor=mesh.shape["tensor"]),
        mesh=mesh,
        in_specs=(
            rows, rows, rows, rows, cols, cols, cols, turned_rows(), cols, cols, cols, turned_rows(), cols,
            turned_rows(), P(), P(), P(), rows,
        ),
        out_specs=(
            rows, both, both, both, both, both, turned, both, both, both, turned, both, turned,
            P(None, "dp"), P(None, "dp"), P(None, "dp"),
        ),
        check_vma=False,
    )


def turned_rows():
    return P("tensor", None)
```

profile of v0, /device:TPU:0, one launch (start us, length us, event | category | flops | bytes accessed | tf_op | source)
XLA Modules:
  0.0 200.3 jit_solution(5855885086457501045)
XLA Ops:
  0.6 1.9 pack_weights.3
  2.6 3.0 %collective-permute-start = (bf16[1024,256]{1,0:T(8,128)(2,1)}, bf16[1024,256]{1,0:T(8,128)(2,1)S(1)}, u32[]{:S(2)}, u32[]{:S(2)}) collective-permute-start(bf16[1024,256]{1,0:T(8,128)(2,1)} %pack_weights.3), channel_id=1, source_target_pairs={{0,1},{1,0},{2,3},{3,2},{4,5},{5,4},{6,7},{7,6},{8,9},{9,8},{10,11... | collective-permute-start | bytes 1572872 | tf_op jit(solution)/shard_map/ppermute | solution.py:964
  5.6 3.4 %pack_weights.2 = (bf16[1024,256]{1,0:T(8,128)(2,1)}, bf16[1024,512]{1,0:T(8,128)(2,1)}, s32[8,1024]{1,0:T(8,128)}, s32[8,128]{1,0:T(8,128)}) custom-call(bf16[512,256]{1,0:T(8,128)(2,1)} %refs_20_.1, bf16[512,256]{1,0:T(8,128)(2,1)} %refs_21_.1, bf16[512,256]{1,0:T(8,128)(2,1)} %refs_22_.1, bf16[256,512]{1,0:T(8,128)(2,1)} %refs_2_.19, ...), custom_call_target="tpu_custom_call" | custom-call | flops 5000000000 | bytes 1024 | tf_op jit(solution)/shard_map/pack_weights/pallas_call | solution.py:911
  10.6 6.7 %self_forward_own.1 = (bf16[1024,256]{1,0:T(8,128)(2,1)S(1)}, bf16[1024,256]{1,0:T(8,128)(2,1)S(1)}, bf16[1024,256]{1,0:T(8,128)(2,1)S(1)}, bf16[1024,256]{1,0:T(8,128)(2,1)S(1)}, f32[4,1024]{1,0:T(4,128)S(1)}) custom-call(s32[8,128]{1,0:T(8,128)S(1)} %copy-done.2, bf16[512,256]{1,0:T(8,128)(2,1)S(1)} %copy-done.28, bf16[512,256]{1,0:T(8,128)(2,1)S(1)} %copy-done.30, ...), custom_call_target="tpu_custom_call" | custom-call | flops 35000000512 | bytes 1024 | tf_op jit(solution)/shard_map/self_forward_own/pallas_call | solution.py:859
  21.7 9.5 %self_forward_rest.1 = (bf16[1024,256]{1,0:T(8,128)(2,1)S(1)}, bf16[1024,256]{1,0:T(8,128)(2,1)S(1)}, bf16[1024,256]{1,0:T(8,128)(2,1)S(1)}, bf16[1024,256]{1,0:...) custom-call(s32[8,128]{1,0:T(8,128)S(1)} %copy-done.3, ...), custom_call_target="tpu_custom_call" | custom-call | flops 40000000000 | bytes 1024 | tf_op jit(solution)/shard_map/self_forward_rest/pallas_call | solution.py:859
  36.2 14.6 %cross_forward.1 = (bf16[1024,256]{1,0:T(8,128)(2,1)S(1)}, bf16[1024,256]{1,0:T(8,128)(2,1)S(1)}, bf16[1024,256]{1,0:T(8,128)(2,1)S(1)}, bf16[1024,256]{1,0:T(8,...) custom-call(s32[8,128]{1,0:T(8,128)S(1)} %copy-done.3, ...), custom_call_target="tpu_custom_call" | custom-call | flops 70000001024 | bytes 1024 | tf_op jit(solution)/shard_map/cross_forward/pallas_call | solution.py:859
  52.6 5.9 %ffn_forward_own.1 = (bf16[1024,1024]{1,0:T(8,128)(2,1)S(1)}, bf16[1024,1024]{1,0:T(8,128)(2,1)S(1)}, f32[1024,512]{1,0:T(8,128)S(1)}) custom-call(s32[8,128]{1,0:T(8,128)S(1)} %copy-done.3, bf16[512,1024]{1,0:T(8,128)(2,1)S(1)} %copy-done.8, f32[3,512]{1,0:T(4,128)S(1)} %copy-done.34, f32[3,512]{1,0:T(4,128)S(1)} %copy-done.35, ...), custom_call_target="tpu_custom_call" | custom-call | flops 40000000000 | bytes 1024 | tf_op jit(solution)/shard_map/ffn_forward_own/pallas_call | solution.py:859
  59.9 2.7 %collective-permute-done.5.refs_1_.refs_10_ = bf16[1024,512]{1,0:T(8,128)(2,1)S(1)} collective-permute-done((bf16[1024,512]{1,0:T(8,128)(2,1)S(1)}, bf16[1024,512]{1,0:T(8,128)(2,1)S(1)}, u32[]{:S(2)}, u32[]{:S(2)}) %collective-permute-start.5) | collective-permute-done | bytes 1048608 | tf_op jit(solution)/shard_map/ppermute | solution.py:1049
  62.5 12.4 %ffn_forward_rest.1 = (bf16[1024,512]{1,0:T(8,128)(2,1)S(1)}, bf16[2048,512]{1,0:T(8,128)(2,1)}, bf16[1024,1024]{1,0:T(8,128)(2,1)S(1)}, f32[1024,512]{1,0:T(8,1...) custom-call(s32[8,128]{1,0:T(8,128)S(1)} %copy-done.3, ...), custom_call_target="tpu_custom_call" | custom-call | flops 54999998464 | bytes 1024 | tf_op jit(solution)/shard_map/ffn_forward_rest/pallas_call | solution.py:859
  75.1 12.3 %ffn_backward.1 = (f32[1024,512]{1,0:T(8,128)S(1)}, bf16[256,2048]{1,0:T(8,128)(2,1)S(1)}, bf16[256,2048]{1,0:T(8,128)(2,1)}, f32[8,512]{1,0:T(8,128)S(1)}) custom-call(s32[8,128]{1,0:T(8,128)S(1)} %copy-done.3, bf16[1024,512]{1,0:T(8,128)(2,1)S(1)} %copy-done.9, bf16[512,1024]{1,0:T(8,128)(2,1)S(1)} %copy-done.8, f32[3,512]{1,0:T(4,128)S(1)} %copy-done.34, ...), custom_call_target="tpu_custom_call" | custom-call | flops 60000002048 | bytes 1024 | tf_op jit(solution)/shard_map/ffn_backward/pallas_call | solution.py:859
  94.0 1.8 collective-permute-start.8
  100.1 30.4 %cross_backward.1 = (f32[1024,512]{1,0:T(8,128)}, f32[2048,256]{1,0:T(8,128)}, bf16[1024,256]{1,0:T(8,128)(2,1)S(1)}, bf16[256,2048]{1,0:T(8,128)(2,1)S(1)}, bf1...) custom-call(s32[8,128]{1,0:T(8,128)S(1)} %copy-done.3, bf16[1024,256]{1,0:T(8,128)(2,1)S(1)} %copy-done.15, ...), custom_call_target="tpu_custom_call" | custom-call | flops 115000000512 | bytes 1024 | tf_op jit(solution)/shard_map/cross_backward/pallas_call | solution.py:859
  132.4 1.8 add_convert_fusion.11
  134.5 1.6 collective-permute-start.14
  136.1 2.5 %collective-permute-start.15 = (bf16[32,4096]{1,0:T(8,128)(2,1)S(1)}, bf16[32,4096]{1,0:T(8,128)(2,1)S(1)}, u32[]{:S(2)}, u32[]{:S(2)}) collective-permute-start(bf16[32,4096]{1,0:T(8,128)(2,1)S(1)} %get-tuple-element.281), channel_id=1, source_target_pairs={{0,16},{2,18},{4,20},{6,22},{8,24},{10,26},{12,28},{14,30},{16,0},... | collective-permute-start | bytes 786440 | tf_op jit(solution)/shard_map/ppermute | solution.py:992
  140.8 15.4 %self_backward.1 = (bf16[1024,256]{1,0:T(8,128)(2,1)S(1)}, bf16[1024,256]{1,0:T(8,128)(2,1)S(1)}, bf16[1024,256]{1,0:T(8,128)(2,1)S(1)}, bf16[1024,256]{1,0:T(8,...) custom-call(s32[8,128]{1,0:T(8,128)S(1)} %copy-done.3, ...), custom_call_target="tpu_custom_call", output_to_operand_aliasing={{8}: (21, {})} | custom-call | flops 80000000000 | bytes 1024 | tf_op jit(solution)/shard_map/self_backward/pallas_call | solution.py:859
  156.8 5.9 %collective-permute-start.20 = (bf16[32,2048]{1,0:T(8,128)(2,1)S(1)}, bf16[32,2048]{1,0:T(8,128)(2,1)S(1)}, u32[]{:S(2)}, u32[]{:S(2)}) collective-permute-start(bf16[32,2048]{1,0:T(8,128)(2,1)S(1)} %get-tuple-element.286), channel_id=1, source_target_pairs={{0,8},{2,10},{4,12},{6,14},{8,16},{10,18},{12,20},{14,22},{16,24},... | collective-permute-start | bytes 393224 | tf_op jit(solution)/shard_map/ppermute | solution.py:992
  169.5 4.6 %input_backward.1 = (f32[2048,256]{1,0:T(8,128)}, bf16[1024,256]{1,0:T(8,128)(2,1)S(1)}, f32[2048,256]{1,0:T(8,128)}) custom-call(s32[8,128]{1,0:T(8,128)S(1)} %copy-done.3, bf16[1024,256]{1,0:T(8,128)(2,1)S(1)} %copy-done.11, bf16[1024,256]{1,0:T(8,128)(2,1)S(1)} %copy-done.13, bf16[512,256]{1,0:T(8,128)(2,1)S(1)} %copy-done.29, ...), custom_call_target="tpu_custom_call", output_to_operand_aliasing={{2}: (15, {})} | custom-call | flops 24999999488 | bytes 1024 | tf_op jit(solution)/shard_map/input_backward/pallas_call | solution.py:859
  176.0 5.3 %collective-permute-done.19 = bf16[128,1152]{1,0:T(8,128)(2,1)S(1)} collective-permute-done((bf16[128,1152]{1,0:T(8,128)(2,1)S(1)}, bf16[128,1152]{1,0:T(8,128)(2,1)S(1)}, u32[]{:S(2)}, u32[]{:S(2)}) %collective-permute-start.19) | collective-permute-done | bytes 294944 | tf_op jit(solution)/shard_map/ppermute | solution.py:1147
  184.0 2.0 collective-permute-start.26
  187.6 2.5 %collective-permute-done.25.refs_4_ = bf16[32,1152]{1,0:T(8,128)(2,1)S(1)} collective-permute-done((bf16[32,1152]{1,0:T(8,128)(2,1)S(1)}, bf16[32,1152]{1,0:T(8,128)(2,1)S(1)}, u32[]{:S(2)}, u32[]{:S(2)}) %collective-permute-start.25) | collective-permute-done | bytes 73760 | tf_op jit(solution)/shard_map/ppermute | solution.py:992
  190.9 2.5 %finish.1 = (f32[32,256]{1,0:T(8,128)}, f32[32,256]{1,0:T(8,128)}, f32[32,256]{1,0:T(8,128)}, f32[32,256]{1,0:T(8,128)}, f32[32,256]{1,0:T(8,128)}, /*index=5*/f...) custom-call(s32[8,128]{1,0:T(8,128)S(1)} %copy-done.3, ...), custom_call_target="tpu_custom_call" | custom-call | flops 50000000 | bytes 1024 | tf_op jit(solution)/shard_map/finish/pallas_call | solution.py:859
  193.4 4.4 %collective-permute-done.23.refs_1_ = bf16[1024,256]{1,0:T(8,128)(2,1)S(1)} collective-permute-done((bf16[1024,256]{1,0:T(8,128)(2,1)S(1)}, bf16[1024,256]{1,0:T(8,128)(2,1)S(1)}, u32[]{:S(2)}, u32[]{:S(2)}) %collective-permute-start.23) | collective-permute-done | bytes 524320 | tf_op jit(solution)/shard_map/ppermute | solution.py:1160
  197.8 2.3 %fill_kernel.1 = f32[2048,256]{1,0:T(8,128)} custom-call(s32[8,128]{1,0:T(8,128)S(1)} %copy-done.3, f32[2048,256]{1,0:T(8,128)} %get-tuple-element.248.refs_0_, bf16[1024,256]{1,0:T(8,128)(2,1)S(1)} %collective-permute-done.23.refs_1_), custom_call_target="tpu_custom_call", output_to_operand_aliasing={{}: (1, {})} | custom-call | flops 5000000000 | bytes 1024 | tf_op jit(solution)/shard_map/fill_kernel/pallas_call | solution.py:859
  (229 shorter events, 43.0 us)
Async XLA Ops:
  2.6 17.2 %collective-permute-start = (bf16[1024,256]{1,0:T(8,128)(2,1)}, bf16[1024,256]{1,0:T(8,128)(2,1)S(1)}, u32[]{:S(2)}, u32[]{:S(2)}) collective-permute-start(bf16[1024,256]{1,0:T(8,128)(2,1)} %pack_weights.3), channel_id=1, source_target_pairs={{0,1},{1,0},{2,3},{3,2},{4,5},{5,4},{6,7},{7,6},{8,9},{9,8},{10,11... | collective-permute-start | bytes 1572872 | tf_op jit(solution)/shard_map/ppermute | solution.py:964
  19.9 14.4 %collective-permute-start.2 = (bf16[1024,256]{1,0:T(8,128)(2,1)S(1)}, bf16[1024,256]{1,0:T(8,128)(2,1)S(1)}, u32[]{:S(2)}, u32[]{:S(2)}) collective-permute-start(bf16[1024,256]{1,0:T(8,128)(2,1)S(1)} %copy-done.82), channel_id=1, source_target_pairs={{0,1},{1,0},{2,3},{3,2},{4,5},{5,4},{6,7},{7,6},{8,9},{9,8},{10,11... | collective-permute-start | bytes 1572872 | tf_op jit(solution)/shard_map/ppermute | solution.py:1020
  34.3 25.6 %collective-permute-start.4 = (bf16[1024,512]{1,0:T(8,128)(2,1)S(1)}, bf16[1024,512]{1,0:T(8,128)(2,1)S(1)}, u32[]{:S(2)}, u32[]{:S(2)}) collective-permute-start(bf16[1024,512]{1,0:T(8,128)(2,1)S(1)} %copy-done.81), channel_id=1, source_target_pairs={{0,1},{1,0},{2,3},{3,2},{4,5},{5,4},{6,7},{7,6},{8,9},{9,8},{10,11... | collective-permute-start | bytes 3145736 | tf_op jit(solution)/shard_map/ppermute | solution.py:1029
  74.9 13.8 %collective-permute-start.6 = (bf16[256,2048]{1,0:T(8,128)(2,1)S(1)}, bf16[256,2048]{1,0:T(8,128)(2,1)S(1)}, u32[]{:S(2)}, u32[]{:S(2)}) collective-permute-start(bf16[256,2048]{1,0:T(8,128)(2,1)S(1)} %get-tuple-element.181), channel_id=1, source_target_pairs={{0,2},{2,0},{4,6},{6,4},{8,10},{10,8},{12,14},{14,12},{16,18},{18,... | collective-permute-start | bytes 3145736 | tf_op jit(solution)/shard_map/ppermute | solution.py:1055
  90.1 40.4 %collective-permute-start.9 = (bf16[1024,512]{1,0:T(8,128)(2,1)S(1)}, bf16[1024,512]{1,0:T(8,128)(2,1)S(1)}, u32[]{:S(2)}, u32[]{:S(2)}) collective-permute-start(bf16[1024,512]{1,0:T(8,128)(2,1)S(1)} %get-tuple-element.205), channel_id=1, source_target_pairs={{0,1},{1,0},{2,3},{3,2},{4,5},{5,4},{6,7},{7,6},{8,9},{9,8},{10,11... | collective-permute-start | bytes 3145736 | tf_op jit(solution)/shard_map/ppermute | solution.py:1067
  94.0 36.5 %collective-permute-start.8 = (bf16[128,4096]{1,0:T(8,128)(2,1)S(1)}, bf16[128,4096]{1,0:T(8,128)(2,1)S(1)}, u32[]{:S(2)}, u32[]{:S(2)}) collective-permute-start(bf16[128,4096]{1,0:T(8,128)(2,1)S(1)} %pad_maximum_fusion), channel_id=1, source_target_pairs={{0,4},{2,6},{4,0},{6,2},{8,12},{10,14},{12,8},{14,10},{16,20},{18,... | collective-permute-start | bytes 3145736 | tf_op jit(solution)/shard_map/ppermute | solution.py:1084
  130.5 9.4 %collective-permute-start.10 = (bf16[256,2048]{1,0:T(8,128)(2,1)S(1)}, bf16[256,2048]{1,0:T(8,128)(2,1)S(1)}, u32[]{:S(2)}, u32[]{:S(2)}) collective-permute-start(bf16[256,2048]{1,0:T(8,128)(2,1)S(1)} %get-tuple-element.208), channel_id=1, source_target_pairs={{0,2},{2,0},{4,6},{6,4},{8,10},{10,8},{12,14},{14,12},{16,18},{18,... | collective-permute-start | bytes 3145736 | tf_op jit(solution)/shard_map/ppermute | solution.py:1055
  131.4 24.8 %collective-permute-start.12 = (bf16[1024,256]{1,0:T(8,128)(2,1)S(1)}, bf16[1024,256]{1,0:T(8,128)(2,1)S(1)}, u32[]{:S(2)}, u32[]{:S(2)}) collective-permute-start(bf16[1024,256]{1,0:T(8,128)(2,1)S(1)} %get-tuple-element.234), channel_id=1, source_target_pairs={{0,1},{1,0},{2,3},{3,2},{4,5},{5,4},{6,7},{7,6},{8,9},{9,8},{10,11... | collective-permute-start | bytes 1572872 | tf_op jit(solution)/shard_map/ppermute | solution.py:1104
  134.5 21.8 %collective-permute-start.14 = (bf16[32,4096]{1,0:T(8,128)(2,1)S(1)}, bf16[32,4096]{1,0:T(8,128)(2,1)S(1)}, u32[]{:S(2)}, u32[]{:S(2)}) collective-permute-start(bf16[32,4096]{1,0:T(8,128)(2,1)S(1)} %get-tuple-element.279), channel_id=1, source_target_pairs={{0,8},{2,10},{4,12},{6,14},{8,16},{10,18},{12,20},{14,22},{16,24},... | collective-permute-start | bytes 786440 | tf_op jit(solution)/shard_map/ppermute | solution.py:992
  136.1 20.2 %collective-permute-start.15 = (bf16[32,4096]{1,0:T(8,128)(2,1)S(1)}, bf16[32,4096]{1,0:T(8,128)(2,1)S(1)}, u32[]{:S(2)}, u32[]{:S(2)}) collective-permute-start(bf16[32,4096]{1,0:T(8,128)(2,1)S(1)} %get-tuple-element.281), channel_id=1, source_target_pairs={{0,16},{2,18},{4,20},{6,22},{8,24},{10,26},{12,28},{14,30},{16,0},... | collective-permute-start | bytes 786440 | tf_op jit(solution)/shard_map/ppermute | solution.py:992
  138.6 17.7 %collective-permute-start.16 = (bf16[32,4096]{1,0:T(8,128)(2,1)S(1)}, bf16[32,4096]{1,0:T(8,128)(2,1)S(1)}, u32[]{:S(2)}, u32[]{:S(2)}) collective-permute-start(bf16[32,4096]{1,0:T(8,128)(2,1)S(1)} %get-tuple-element.280), channel_id=1, source_target_pairs={{0,24},{2,26},{4,28},{6,30},{8,0},{10,2},{12,4},{14,6},{16,8},{18,... | collective-permute-start | bytes 786440 | tf_op jit(solution)/shard_map/ppermute | solution.py:992
  140.1 16.1 %collective-permute-start.11 = (bf16[128,2048]{1,0:T(8,128)(2,1)S(1)}, bf16[128,2048]{1,0:T(8,128)(2,1)S(1)}, u32[]{:S(2)}, u32[]{:S(2)}) collective-permute-start(bf16[128,2048]{1,0:T(8,128)(2,1)S(1)} %add_convert_fusion.1), channel_id=1, source_target_pairs={{0,4},{2,6},{4,0},{6,2},{8,12},{10,14},{12,8},{14,10},{16,20},{18,... | collective-permute-start | bytes 1572872 | tf_op jit(solution)/shard_map/ppermute | solution.py:1121
  156.2 8.9 %collective-permute-start.13 = (bf16[512,1152]{1,0:T(8,128)(2,1)S(1)}, bf16[512,1152]{1,0:T(8,128)(2,1)S(1)}, u32[]{:S(2)}, u32[]{:S(2)}) collective-permute-start(bf16[512,1152]{1,0:T(8,128)(2,1)S(1)} %get-tuple-element.238), channel_id=1, source_target_pairs={{0,2},{2,0},{4,6},{6,4},{8,10},{10,8},{12,14},{14,12},{16,18},{18,... | collective-permute-start | bytes 3538952 | tf_op jit(solution)/shard_map/ppermute | solution.py:1055
  156.8 11.1 %collective-permute-start.20 = (bf16[32,2048]{1,0:T(8,128)(2,1)S(1)}, bf16[32,2048]{1,0:T(8,128)(2,1)S(1)}, u32[]{:S(2)}, u32[]{:S(2)}) collective-permute-start(bf16[32,2048]{1,0:T(8,128)(2,1)S(1)} %get-tuple-element.286), channel_id=1, source_target_pairs={{0,8},{2,10},{4,12},{6,14},{8,16},{10,18},{12,20},{14,22},{16,24},... | collective-permute-start | bytes 393224 | tf_op jit(solution)/shard_map/ppermute | solution.py:992
  162.7 11.5 %collective-permute-start.21 = (bf16[32,2048]{1,0:T(8,128)(2,1)S(1)}, bf16[32,2048]{1,0:T(8,128)(2,1)S(1)}, u32[]{:S(2)}, u32[]{:S(2)}) collective-permute-start(bf16[32,2048]{1,0:T(8,128)(2,1)S(1)} %get-tuple-element.285), channel_id=1, source_target_pairs={{0,16},{2,18},{4,20},{6,22},{8,24},{10,26},{12,28},{14,30},{16,0},... | collective-permute-start | bytes 393224 | tf_op jit(solution)/shard_map/ppermute | solution.py:992
  164.3 9.9 %collective-permute-start.22 = (bf16[32,2048]{1,0:T(8,128)(2,1)S(1)}, bf16[32,2048]{1,0:T(8,128)(2,1)S(1)}, u32[]{:S(2)}, u32[]{:S(2)}) collective-permute-start(bf16[32,2048]{1,0:T(8,128)(2,1)S(1)} %get-tuple-element.284), channel_id=1, source_target_pairs={{0,24},{2,26},{4,28},{6,30},{8,0},{10,2},{12,4},{14,6},{16,8},{18,... | collective-permute-start | bytes 393224 | tf_op jit(solution)/shard_map/ppermute | solution.py:992
  165.3 9.1 %collective-permute-start.17 = (bf16[128,1152]{1,0:T(8,128)(2,1)S(1)}, bf16[128,1152]{1,0:T(8,128)(2,1)S(1)}, u32[]{:S(2)}, u32[]{:S(2)}) collective-permute-start(bf16[128,1152]{1,0:T(8,128)(2,1)S(1)} %get-tuple-element.278), channel_id=1, source_target_pairs={{0,1},{1,0},{2,3},{3,2},{4,5},{5,4},{6,7},{7,6},{8,9},{9,8},{10,11... | collective-permute-start | bytes 884744 | tf_op jit(solution)/shard_map/ppermute | solution.py:1146
  166.1 9.9 %collective-permute-start.18 = (bf16[128,1152]{1,0:T(8,128)(2,1)S(1)}, bf16[128,1152]{1,0:T(8,128)(2,1)S(1)}, u32[]{:S(2)}, u32[]{:S(2)}) collective-permute-start(bf16[128,1152]{1,0:T(8,128)(2,1)S(1)} %get-tuple-element.277), channel_id=1, source_target_pairs={{0,4},{2,6},{4,0},{6,2},{8,12},{10,14},{12,8},{14,10},{16,20},{18,... | collective-permute-start | bytes 884744 | tf_op jit(solution)/shard_map/ppermute | solution.py:1146
  167.9 13.4 %collective-permute-start.19 = (bf16[128,1152]{1,0:T(8,128)(2,1)S(1)}, bf16[128,1152]{1,0:T(8,128)(2,1)S(1)}, u32[]{:S(2)}, u32[]{:S(2)}) collective-permute-start(bf16[128,1152]{1,0:T(8,128)(2,1)S(1)} %get-tuple-element.276), channel_id=1, source_target_pairs={{0,5},{1,4},{2,7},{3,6},{4,1},{5,0},{6,3},{7,2},{8,13},{9,12},{10,... | collective-permute-start | bytes 884744 | tf_op jit(solution)/shard_map/ppermute | solution.py:1147
  181.4 9.5 %collective-permute-start.24 = (bf16[32,3072]{1,0:T(8,128)(2,1)S(1)}, bf16[32,3072]{1,0:T(8,128)(2,1)S(1)}, u32[]{:S(2)}, u32[]{:S(2)}) collective-permute-start(bf16[32,3072]{1,0:T(8,128)(2,1)S(1)} %pad_maximum_fusion.2), channel_id=1, source_target_pairs={{0,1},{1,0},{2,3},{3,2},{4,5},{5,4},{6,7},{7,6},{8,9},{9,8},{10,11... | collective-permute-start | bytes 589832 | tf_op jit(solution)/shard_map/ppermute | solution.py:1163
  182.1 15.6 %collective-permute-start.23 = (bf16[1024,256]{1,0:T(8,128)(2,1)S(1)}, bf16[1024,256]{1,0:T(8,128)(2,1)S(1)}, u32[]{:S(2)}, u32[]{:S(2)}) collective-permute-start(bf16[1024,256]{1,0:T(8,128)(2,1)S(1)} %get-tuple-element.250), channel_id=1, source_target_pairs={{0,1},{1,0},{2,3},{3,2},{4,5},{5,4},{6,7},{7,6},{8,9},{9,8},{10,11... | collective-permute-start | bytes 1572872 | tf_op jit(solution)/shard_map/ppermute | solution.py:1160
  183.7 6.3 %collective-permute-start.25 = (bf16[32,1152]{1,0:T(8,128)(2,1)S(1)}, bf16[32,1152]{1,0:T(8,128)(2,1)S(1)}, u32[]{:S(2)}, u32[]{:S(2)}) collective-permute-start(bf16[32,1152]{1,0:T(8,128)(2,1)S(1)} %get-tuple-element.290), channel_id=1, source_target_pairs={{0,8},{2,10},{4,12},{6,14},{8,16},{10,18},{12,20},{14,22},{16,24},... | collective-permute-start | bytes 221192 | tf_op jit(solution)/shard_map/ppermute | solution.py:992
  184.0 6.8 %collective-permute-start.26 = (bf16[32,1152]{1,0:T(8,128)(2,1)S(1)}, bf16[32,1152]{1,0:T(8,128)(2,1)S(1)}, u32[]{:S(2)}, u32[]{:S(2)}) collective-permute-start(bf16[32,1152]{1,0:T(8,128)(2,1)S(1)} %get-tuple-element.289), channel_id=1, source_target_pairs={{0,16},{2,18},{4,20},{6,22},{8,24},{10,26},{12,28},{14,30},{16,0},... | collective-permute-start | bytes 221192 | tf_op jit(solution)/shard_map/ppermute | solution.py:992
  186.0 4.8 %collective-permute-start.27 = (bf16[32,1152]{1,0:T(8,128)(2,1)S(1)}, bf16[32,1152]{1,0:T(8,128)(2,1)S(1)}, u32[]{:S(2)}, u32[]{:S(2)}) collective-permute-start(bf16[32,1152]{1,0:T(8,128)(2,1)S(1)} %get-tuple-element.288), channel_id=1, source_target_pairs={{0,24},{2,26},{4,28},{6,30},{8,0},{10,2},{12,4},{14,6},{16,8},{18,... | collective-permute-start | bytes 221192 | tf_op jit(solution)/shard_map/ppermute | solution.py:992
  (88 other events, 891.7 us)
where the time goes:
time: 204 us; the launch traced here: 200 us
  Pallas kernels  122 us (60%)
  starting transfers between devices  31.5 us (15%)
  waiting for transfers between devices  25.4 us (12%)
  local copies, waits for them, and re-layouts  14.1 us (7%)
  other arithmetic  5.41 us (3%)
    pallas_call x11, Pallas kernels, call(): pl.pallas_call(kernel, out_shape=[jax.ShapeDtypeStruct(shape, kind) for s...  117 us
    ppermute x9, starting transfers between devices, z_send(): parts.append(lax.ppermute(out, 'dp', perm))  17.6 us
    unnamed x166, local copies, waits for them, and re-layouts  13.9 us
    pallas_call x2, Pallas kernels, pack(): pl.pallas_call(pack_weights, out_shape=[jax.ShapeDtypeStruct(shape, kind)...  5.31 us
    ppermute x1, waiting for transfers between devices, local(): lax.ppermute(s_near[2], ('dp', 'tensor'), across)  5.27 us
    convert_element_type x7, other arithmetic, part_total(): total(*[array[n * size:(n + 1) * size] for array in arrays]).astype(BF16)  5.05 us
    ppermute x9, waiting for transfers between devices, z_send(): parts.append(lax.ppermute(out, 'dp', perm))  4.52 us
    ppermute x1, waiting for transfers between devices, local(): in_other = lax.ppermute(in_send, 'tensor', swap_y)  4.37 us
  transfers between devices with their start and end apart: 28, of which 13 were waited for; matrix products, arithmetic and copies ran while one was open for 3% of the time, Pallas kernels for 53%

commit v1 on v0

--- a/solution.py
+++ b/solution.py
@@ -573,13 +573,12 @@
     qx, kx, vx, ox, do, do_x, delta, delta_x, dq, dq_x, dk, dk_x, dv, dv_x, dkb, dkb_x, dvb, dvb_x, r_scr,
     grad_t, norm_t, mem_t, acc, grads, *, chunk,
 ):
+    half = qo.shape[1]
+    blocks = mem.shape[0] // QB
+    for ref in (sums, dk, dk_x, dv, dv_x):
+        ref[...] = jnp.zeros_like(ref)
     need(mine, sib, oo, gain, shift, omega)
     unpack_square(mine, sib, (qx, kx, vx, ox))
-    sums[...] = jnp.zeros_like(sums)
-    half = qo.shape[1]
-    blocks = mem.shape[0] // QB
-    for ref in (dk, dk_x, dv, dv_x):
-        ref[...] = jnp.zeros_like(ref)
 
     @pl.loop(0, mem.chunks)
     def _(i):
@@ -647,11 +646,11 @@
     dq, dq_x, dkb, dkb_x, dvb, dvb_x, keep, send, out_all,
     qx, kx, vx, ox, do, do_x, delta, delta_x, dk, dk_x, dv, dv_x, r_scr, grad_t, in_t, sums, all_sums, sums_t, grads, *, chunk,
 ):
-    need(mine, sib, oo)
-    unpack_square(mine, sib, (qx, kx, vx, ox))
     blocks = x.shape[0] // QB
     for ref in (sums, all_sums, dk, dk_x, dv, dv_x):
         ref[...] = jnp.zeros_like(ref)
+    need(mine, sib, oo)
+    unpack_square(mine, sib, (qx, kx, vx, ox))
 
     @pl.loop(0, x.chunks)
     def _(i):
@@ -1096,7 +1095,7 @@
              *[(side, BF16)] * 4, ((2, heads * QB, GW), F32), turned, turned, turned, block_wide,
              ((model, 8 * half), BF16)],
             23, {8: (length, False)}, {1: (length, False)}, cuts={n: cut for n in range(6, 11)},
-            out_cuts={n: cut for n in range(3)}, bare=(3, 4), dealt=dealt,
+            out_cuts={n: cut for n in range(3)}, bare=(3, 4), dealt=dealt, full=True,
         ),
         f_x, out_other,
     ))
@@ -1146,7 +1145,6 @@
             lax.ppermute(s_near[0], "tensor", swap_y), lax.ppermute(s_near[1], "dp", swap(2)),
             lax.ppermute(s_near[2], ("dp", "tensor"), across),
         ]
-        c_z = z_send(c_part)
     input_grad, in_send, memory_grad = call(
         input_backward, sc,
         [mine_s, sib_s, *own_s[:3], residual_scale, d_pre1, *d_self, mem_other, memory_grad],
@@ -1156,8 +1154,10 @@
     thin, broad = ((chunk, half), F32), ((chunk, hidden), F32)
     three = ((3, chunk), F32)
     if dealt:
-        in_send, s_near, c_z = lax.optimization_barrier((in_send, s_near, c_z))
+        in_send, c_part = lax.optimization_barrier((in_send, c_part))
         in_other = lax.ppermute(in_send, "tensor", swap_y)
+        c_z = z_send(c_part)
+        in_other, c_z = lax.optimization_barrier((in_other, c_z))
         s_far = z_send(part_total(0, s_keep, s_other, *s_near))
         c_last = total(*c_z).astype(BF16)
         late = lax.ppermute(

time: 204 us -> 199 us (0.975)
  the two profiles are of different devices: /device:TPU:0 before, /device:TPU:8 now
where the time goes in v1:
time: 199 us; the launch traced here: 196 us
  Pallas kernels  124 us (62%)
  waiting for transfers between devices  31.7 us (16%)
  starting transfers between devices  22.3 us (11%)
  local copies, waits for them, and re-layouts  10.5 us (5%)
  other arithmetic  5.79 us (3%)
    pallas_call x11, Pallas kernels, call(): pl.pallas_call(kernel, out_shape=[jax.ShapeDtypeStruct(shape, kind) for s...  118 us
    ppermute x9, waiting for transfers between devices, z_send(): parts.append(lax.ppermute(out, 'dp', perm))  11.8 us
    ppermute x9, starting transfers between devices, z_send(): parts.append(lax.ppermute(out, 'dp', perm))  11 us
    unnamed x146, local copies, waits for them, and re-layouts  10.4 us
    convert_element_type x7, other arithmetic, part_total(): total(*[array[n * size:(n + 1) * size] for array in arrays]).astype(BF16)  5.41 us
    pallas_call x2, Pallas kernels, pack(): pl.pallas_call(pack_weights, out_shape=[jax.ShapeDtypeStruct(shape, kind)...  5.31 us
    ppermute x1, waiting for transfers between devices, local(): lax.ppermute(s_near[2], ('dp', 'tensor'), across)  4.62 us
    ppermute x1, waiting for transfers between devices, local(): lax.ppermute(jnp.concatenate([f_last[:, 2 * hidden:], c_last[:, 4 * half:...  4.18 us
  transfers between devices with their start and end apart: 28, of which 14 were waited for; matrix products, arithmetic and copies ran while one was open for 3% of the time, Pallas kernels for 54%

profile of v1, /device:TPU:8, one launch (start us, length us, event | category | flops | bytes accessed | tf_op | source)
XLA Modules:
  0.0 195.9 jit_solution(1148436085243116772)
XLA Ops:
  4.2 3.4 %pack_weights.2 = (bf16[1024,256]{1,0:T(8,128)(2,1)}, bf16[1024,512]{1,0:T(8,128)(2,1)}, s32[8,1024]{1,0:T(8,128)}, s32[8,128]{1,0:T(8,128)}) custom-call(bf16[512,256]{1,0:T(8,128)(2,1)} %refs_20_.1, bf16[512,256]{1,0:T(8,128)(2,1)} %refs_21_.1, bf16[512,256]{1,0:T(8,128)(2,1)} %refs_22_.1, bf16[256,512]{1,0:T(8,128)(2,1)} %refs_2_.19, ...), custom_call_target="tpu_custom_call" | custom-call | flops 5000000000 | bytes 1024 | tf_op jit(solution)/shard_map/pack_weights/pallas_call | solution.py:910
  9.1 6.7 %self_forward_own.1 = (bf16[1024,256]{1,0:T(8,128)(2,1)S(1)}, bf16[1024,256]{1,0:T(8,128)(2,1)S(1)}, bf16[1024,256]{1,0:T(8,128)(2,1)S(1)}, bf16[1024,256]{1,0:T(8,128)(2,1)S(1)}, f32[4,1024]{1,0:T(4,128)S(1)}) custom-call(s32[8,128]{1,0:T(8,128)S(1)} %copy-done.2, bf16[512,256]{1,0:T(8,128)(2,1)S(1)} %copy-done.23, bf16[512,256]{1,0:T(8,128)(2,1)S(1)} %copy-done.25, ...), custom_call_target="tpu_custom_call" | custom-call | flops 35000000512 | bytes 1024 | tf_op jit(solution)/shard_map/self_forward_own/pallas_call | solution.py:858
  20.2 9.5 %self_forward_rest.1 = (bf16[1024,256]{1,0:T(8,128)(2,1)S(1)}, bf16[1024,256]{1,0:T(8,128)(2,1)S(1)}, bf16[1024,256]{1,0:T(8,128)(2,1)S(1)}, bf16[1024,256]{1,0:...) custom-call(s32[8,128]{1,0:T(8,128)S(1)} %copy-done.3, ...), custom_call_target="tpu_custom_call" | custom-call | flops 40000000000 | bytes 1024 | tf_op jit(solution)/shard_map/self_forward_rest/pallas_call | solution.py:858
  34.7 14.6 %cross_forward.1 = (bf16[1024,256]{1,0:T(8,128)(2,1)S(1)}, bf16[1024,256]{1,0:T(8,128)(2,1)S(1)}, bf16[1024,256]{1,0:T(8,128)(2,1)S(1)}, bf16[1024,256]{1,0:T(8,...) custom-call(s32[8,128]{1,0:T(8,128)S(1)} %copy-done.3, ...), custom_call_target="tpu_custom_call" | custom-call | flops 70000001024 | bytes 1024 | tf_op jit(solution)/shard_map/cross_forward/pallas_call | solution.py:858
  51.7 5.9 %ffn_forward_own.1 = (bf16[1024,1024]{1,0:T(8,128)(2,1)S(1)}, bf16[1024,1024]{1,0:T(8,128)(2,1)S(1)}, f32[1024,512]{1,0:T(8,128)S(1)}) custom-call(s32[8,128]{1,0:T(8,128)S(1)} %copy-done.3, bf16[512,1024]{1,0:T(8,128)(2,1)S(1)} %copy-done.9, f32[3,512]{1,0:T(4,128)S(1)} %copy-done.29, f32[3,512]{1,0:T(4,128)S(1)} %copy-done.30, ...), custom_call_target="tpu_custom_call" | custom-call | flops 40000000000 | bytes 1024 | tf_op jit(solution)/shard_map/ffn_forward_own/pallas_call | solution.py:858
  58.4 2.7 %collective-permute-done.5.refs_1_.refs_10_ = bf16[1024,512]{1,0:T(8,128)(2,1)S(1)} collective-permute-done((bf16[1024,512]{1,0:T(8,128)(2,1)S(1)}, bf16[1024,512]{1,0:T(8,128)(2,1)S(1)}, u32[]{:S(2)}, u32[]{:S(2)}) %collective-permute-start.5) | collective-permute-done | bytes 1048608 | tf_op jit(solution)/shard_map/ppermute | solution.py:1048
  61.0 12.4 %ffn_forward_rest.1 = (bf16[1024,512]{1,0:T(8,128)(2,1)S(1)}, bf16[2048,512]{1,0:T(8,128)(2,1)}, bf16[1024,1024]{1,0:T(8,128)(2,1)S(1)}, f32[1024,512]{1,0:T(8,1...) custom-call(s32[8,128]{1,0:T(8,128)S(1)} %copy-done.3, ...), custom_call_target="tpu_custom_call" | custom-call | flops 54999998464 | bytes 1024 | tf_op jit(solution)/shard_map/ffn_forward_rest/pallas_call | solution.py:858
  73.6 12.3 %ffn_backward.1 = (f32[1024,512]{1,0:T(8,128)S(1)}, bf16[256,2048]{1,0:T(8,128)(2,1)S(1)}, bf16[256,2048]{1,0:T(8,128)(2,1)}, f32[8,512]{1,0:T(8,128)S(1)}) custom-call(s32[8,128]{1,0:T(8,128)S(1)} %copy-done.3, bf16[1024,512]{1,0:T(8,128)(2,1)S(1)} %copy-done.10, bf16[512,1024]{1,0:T(8,128)(2,1)S(1)} %copy-done.9, f32[3,512]{1,0:T(4,128)S(1)} %copy-done.29, ...), custom_call_target="tpu_custom_call" | custom-call | flops 60000002048 | bytes 1024 | tf_op jit(solution)/shard_map/ffn_backward/pallas_call | solution.py:858
  94.1 31.9 %cross_backward.1 = (f32[1024,512]{1,0:T(8,128)}, f32[2048,256]{1,0:T(8,128)}, bf16[1024,256]{1,0:T(8,128)(2,1)}, bf16[256,2048]{1,0:T(8,128)(2,1)}, bf16[256,2048]{1,0:T(8,128)(2,1)}, /*index=5*/f32[8,512]{1,0:T(8,128)}) custom-call(s32[8,128]{1,0:T(8,128)} %get-tuple-element.143.sc, bf16[1024,256]{1,0:T(8,128)(2,1)} %copy-done.15, ...), custom_call_target="tpu_custom_call" | custom-call | flops 115000000512 | bytes 1024 | tf_op jit(solution)/shard_map/cross_backward/pallas_call | solution.py:858
  126.2 2.3 %add_convert_fusion.11 = (bf16[128,1024]{1,0:T(8,128)(2,1)S(1)}, bf16[128,1024]{1,0:T(8,128)(2,1)S(1)}, bf16[128,1024]{1,0:T(8,128)(2,1)S(1)}, bf16[128,1024]{1,0:T(8,128)(2,1)S(1)}) fusion(bf16[128,4096]{1,0:T(8,128)(2,1)} %collective-permute-done.8, bf16[256,2048]{1,0:T(8,128)(2,1)} %copy-done.70, bf16[256,2048]{1,0:T(8,128)(2,1)S(1)} %get-tuple-element.182, ...), kind=kLoop, calls=%fused_computation.17 | loop fusion | flops 3145728 | bytes 4194304 | tf_op jit(solution)/shard_map/convert_element_type | solution.py:981
  128.8 4.2 %collective-permute-start.14 = (bf16[32,4096]{1,0:T(8,128)(2,1)S(1)}, bf16[32,4096]{1,0:T(8,128)(2,1)S(1)}, u32[]{:S(2)}, u32[]{:S(2)}) collective-permute-start(bf16[32,4096]{1,0:T(8,128)(2,1)S(1)} %get-tuple-element.277), channel_id=1, source_target_pairs={{0,8},{2,10},{4,12},{6,14},{8,16},{10,18},{12,20},{14,22},{16,24},... | collective-permute-start | bytes 786440 | tf_op jit(solution)/shard_map/ppermute | solution.py:991
  137.1 15.4 %self_backward.1 = (bf16[1024,256]{1,0:T(8,128)(2,1)S(1)}, bf16[1024,256]{1,0:T(8,128)(2,1)S(1)}, bf16[1024,256]{1,0:T(8,128)(2,1)S(1)}, bf16[1024,256]{1,0:T(8,...) custom-call(s32[8,128]{1,0:T(8,128)S(1)} %copy-done.4, ...), custom_call_target="tpu_custom_call", output_to_operand_aliasing={{8}: (21, {})} | custom-call | flops 80000000000 | bytes 1024 | tf_op jit(solution)/shard_map/self_backward/pallas_call | solution.py:858
  152.7 2.7 %collective-permute-done.15 = bf16[32,4096]{1,0:T(8,128)(2,1)S(1)} collective-permute-done((bf16[32,4096]{1,0:T(8,128)(2,1)S(1)}, bf16[32,4096]{1,0:T(8,128)(2,1)S(1)}, u32[]{:S(2)}, u32[]{:S(2)}) %collective-permute-start.15) | collective-permute-done | bytes 262176 | tf_op jit(solution)/shard_map/ppermute | solution.py:991
  155.4 2.2 %collective-permute-done.16 = bf16[32,4096]{1,0:T(8,128)(2,1)S(1)} collective-permute-done((bf16[32,4096]{1,0:T(8,128)(2,1)S(1)}, bf16[32,4096]{1,0:T(8,128)(2,1)S(1)}, u32[]{:S(2)}, u32[]{:S(2)}) %collective-permute-start.16) | collective-permute-done | bytes 262176 | tf_op jit(solution)/shard_map/ppermute | solution.py:991
  159.4 2.5 %collective-permute-start.24 = (bf16[128,1152]{1,0:T(8,128)(2,1)S(1)}, bf16[128,1152]{1,0:T(8,128)(2,1)S(1)}, u32[]{:S(2)}, u32[]{:S(2)}) collective-permute-start(bf16[128,1152]{1,0:T(8,128)(2,1)S(1)} %get-tuple-element.274), channel_id=1, source_target_pairs={{0,5},{1,4},{2,7},{3,6},{4,1},{5,0},{6,3},{7,2},{8,13},{9,12},{10,... | collective-permute-start | bytes 884744 | tf_op jit(solution)/shard_map/ppermute | solution.py:1146
  162.0 4.6 %input_backward.1 = (f32[2048,256]{1,0:T(8,128)}, bf16[1024,256]{1,0:T(8,128)(2,1)S(1)}, f32[2048,256]{1,0:T(8,128)}) custom-call(s32[8,128]{1,0:T(8,128)S(1)} %copy-done.4, bf16[1024,256]{1,0:T(8,128)(2,1)S(1)} %copy-done.12, bf16[1024,256]{1,0:T(8,128)(2,1)S(1)} %copy-done.14, bf16[512,256]{1,0:T(8,128)(2,1)S(1)} %copy-done.24, ...), custom_call_target="tpu_custom_call", output_to_operand_aliasing={{2}: (15, {})} | custom-call | flops 24999999488 | bytes 1024 | tf_op jit(solution)/shard_map/input_backward/pallas_call | solution.py:858
  168.0 1.9 collective-permute-start.20
  170.4 4.6 %collective-permute-done.24 = bf16[128,1152]{1,0:T(8,128)(2,1)S(1)} collective-permute-done((bf16[128,1152]{1,0:T(8,128)(2,1)S(1)}, bf16[128,1152]{1,0:T(8,128)(2,1)S(1)}, u32[]{:S(2)}, u32[]{:S(2)}) %collective-permute-start.24) | collective-permute-done | bytes 294944 | tf_op jit(solution)/shard_map/ppermute | solution.py:1146
  176.1 3.8 %collective-permute-done.19 = bf16[32,2048]{1,0:T(8,128)(2,1)S(1)} collective-permute-done((bf16[32,2048]{1,0:T(8,128)(2,1)S(1)}, bf16[32,2048]{1,0:T(8,128)(2,1)S(1)}, u32[]{:S(2)}, u32[]{:S(2)}) %collective-permute-start.19) | collective-permute-done | bytes 131104 | tf_op jit(solution)/shard_map/ppermute | solution.py:991
  180.3 2.3 %collective-permute-done.20 = bf16[32,2048]{1,0:T(8,128)(2,1)S(1)} collective-permute-done((bf16[32,2048]{1,0:T(8,128)(2,1)S(1)}, bf16[32,2048]{1,0:T(8,128)(2,1)S(1)}, u32[]{:S(2)}, u32[]{:S(2)}) %collective-permute-start.20) | collective-permute-done | bytes 131104 | tf_op jit(solution)/shard_map/ppermute | solution.py:991
  182.5 3.6 %collective-permute-done.17.refs_1_ = bf16[1024,256]{1,0:T(8,128)(2,1)S(1)} collective-permute-done((bf16[1024,256]{1,0:T(8,128)(2,1)S(1)}, bf16[1024,256]{1,0:T(8,128)(2,1)S(1)}, u32[]{:S(2)}, u32[]{:S(2)}) %collective-permute-start.17) | collective-permute-done | bytes 524320 | tf_op jit(solution)/shard_map/ppermute | solution.py:1158
  186.6 2.3 %fill_kernel.1 = f32[2048,256]{1,0:T(8,128)} custom-call(s32[8,128]{1,0:T(8,128)S(1)} %copy-done.4, f32[2048,256]{1,0:T(8,128)} %get-tuple-element.247.refs_0_, bf16[1024,256]{1,0:T(8,128)(2,1)S(1)} %collective-permute-done.17.refs_1_), custom_call_target="tpu_custom_call", output_to_operand_aliasing={{}: (1, {})} | custom-call | flops 5000000000 | bytes 1024 | tf_op jit(solution)/shard_map/fill_kernel/pallas_call | solution.py:858
  189.0 4.2 %collective-permute-done.21.refs_2_ = bf16[32,3072]{1,0:T(8,128)(2,1)S(1)} collective-permute-done((bf16[32,3072]{1,0:T(8,128)(2,1)S(1)}, bf16[32,3072]{1,0:T(8,128)(2,1)S(1)}, u32[]{:S(2)}, u32[]{:S(2)}) %collective-permute-start.21) | collective-permute-done | bytes 196640 | tf_op jit(solution)/shard_map/ppermute | solution.py:1163
  193.2 2.5 %finish.1 = (f32[32,256]{1,0:T(8,128)}, f32[32,256]{1,0:T(8,128)}, f32[32,256]{1,0:T(8,128)}, f32[32,256]{1,0:T(8,128)}, f32[32,256]{1,0:T(8,128)}, /*index=5*/f...) custom-call(s32[8,128]{1,0:T(8,128)S(1)} %copy-done.4, ...), custom_call_target="tpu_custom_call" | custom-call | flops 50000000 | bytes 1024 | tf_op jit(solution)/shard_map/finish/pallas_call | solution.py:858
  (209 shorter events, 35.1 us)
Async XLA Ops:
  2.6 15.7 %collective-permute-start = (bf16[1024,256]{1,0:T(8,128)(2,1)}, bf16[1024,256]{1,0:T(8,128)(2,1)S(1)}, u32[]{:S(2)}, u32[]{:S(2)}) collective-permute-start(bf16[1024,256]{1,0:T(8,128)(2,1)} %pack_weights.3), channel_id=1, source_target_pairs={{0,1},{1,0},{2,3},{3,2},{4,5},{5,4},{6,7},{7,6},{8,9},{9,8},{10,11... | collective-permute-start | bytes 1572872 | tf_op jit(solution)/shard_map/ppermute | solution.py:963
  18.4 14.4 %collective-permute-start.2 = (bf16[1024,256]{1,0:T(8,128)(2,1)S(1)}, bf16[1024,256]{1,0:T(8,128)(2,1)S(1)}, u32[]{:S(2)}, u32[]{:S(2)}) collective-permute-start(bf16[1024,256]{1,0:T(8,128)(2,1)S(1)} %copy-done.72), channel_id=1, source_target_pairs={{0,1},{1,0},{2,3},{3,2},{4,5},{5,4},{6,7},{7,6},{8,9},{9,8},{10,11... | collective-permute-start | bytes 1572872 | tf_op jit(solution)/shard_map/ppermute | solution.py:1019
  32.8 25.6 %collective-permute-start.4 = (bf16[1024,512]{1,0:T(8,128)(2,1)S(1)}, bf16[1024,512]{1,0:T(8,128)(2,1)S(1)}, u32[]{:S(2)}, u32[]{:S(2)}) collective-permute-start(bf16[1024,512]{1,0:T(8,128)(2,1)S(1)} %copy-done.71), channel_id=1, source_target_pairs={{0,1},{1,0},{2,3},{3,2},{4,5},{5,4},{6,7},{7,6},{8,9},{9,8},{10,11... | collective-permute-start | bytes 3145736 | tf_op jit(solution)/shard_map/ppermute | solution.py:1028
  73.4 13.8 %collective-permute-start.6 = (bf16[256,2048]{1,0:T(8,128)(2,1)S(1)}, bf16[256,2048]{1,0:T(8,128)(2,1)S(1)}, u32[]{:S(2)}, u32[]{:S(2)}) collective-permute-start(bf16[256,2048]{1,0:T(8,128)(2,1)S(1)} %get-tuple-element.180), channel_id=1, source_target_pairs={{0,2},{2,0},{4,6},{6,4},{8,10},{10,8},{12,14},{14,12},{16,18},{18,... | collective-permute-start | bytes 3145736 | tf_op jit(solution)/shard_map/ppermute | solution.py:1054
  88.6 37.4 %collective-permute-start.9 = (bf16[1024,512]{1,0:T(8,128)(2,1)S(1)}, bf16[1024,512]{1,0:T(8,128)(2,1)S(1)}, u32[]{:S(2)}, u32[]{:S(2)}) collective-permute-start(bf16[1024,512]{1,0:T(8,128)(2,1)S(1)} %get-tuple-element.204), channel_id=1, source_target_pairs={{0,1},{1,0},{2,3},{3,2},{4,5},{5,4},{6,7},{7,6},{8,9},{9,8},{10,11... | collective-permute-start | bytes 3145736 | tf_op jit(solution)/shard_map/ppermute | solution.py:1066
  92.5 33.6 %collective-permute-start.8 = (bf16[128,4096]{1,0:T(8,128)(2,1)S(1)}, bf16[128,4096]{1,0:T(8,128)(2,1)}, u32[]{:S(2)}, u32[]{:S(2)}) collective-permute-start(bf16[128,4096]{1,0:T(8,128)(2,1)S(1)} %pad_maximum_fusion), channel_id=1, source_target_pairs={{0,4},{2,6},{4,0},{6,2},{8,12},{10,14},{12,8},{14,10},{16,20},{18,... | collective-permute-start | bytes 3145736 | tf_op jit(solution)/shard_map/ppermute | solution.py:1083
  126.0 10.1 %collective-permute-start.10 = (bf16[256,2048]{1,0:T(8,128)(2,1)}, bf16[256,2048]{1,0:T(8,128)(2,1)S(1)}, u32[]{:S(2)}, u32[]{:S(2)}) collective-permute-start(bf16[256,2048]{1,0:T(8,128)(2,1)} %get-tuple-element.207), channel_id=1, source_target_pairs={{0,2},{2,0},{4,6},{6,4},{8,10},{10,8},{12,14},{14,12},{16,18},{18,... | collective-permute-start | bytes 3145736 | tf_op jit(solution)/shard_map/ppermute | solution.py:1054
  126.2 26.4 %collective-permute-start.12 = (bf16[1024,256]{1,0:T(8,128)(2,1)}, bf16[1024,256]{1,0:T(8,128)(2,1)S(1)}, u32[]{:S(2)}, u32[]{:S(2)}) collective-permute-start(bf16[1024,256]{1,0:T(8,128)(2,1)} %get-tuple-element.233), channel_id=1, source_target_pairs={{0,1},{1,0},{2,3},{3,2},{4,5},{5,4},{6,7},{7,6},{8,9},{9,8},{10,11... | collective-permute-start | bytes 1572872 | tf_op jit(solution)/shard_map/ppermute | solution.py:1103
  128.8 23.9 %collective-permute-start.14 = (bf16[32,4096]{1,0:T(8,128)(2,1)S(1)}, bf16[32,4096]{1,0:T(8,128)(2,1)S(1)}, u32[]{:S(2)}, u32[]{:S(2)}) collective-permute-start(bf16[32,4096]{1,0:T(8,128)(2,1)S(1)} %get-tuple-element.277), channel_id=1, source_target_pairs={{0,8},{2,10},{4,12},{6,14},{8,16},{10,18},{12,20},{14,22},{16,24},... | collective-permute-start | bytes 786440 | tf_op jit(solution)/shard_map/ppermute | solution.py:991
  133.0 22.4 %collective-permute-start.15 = (bf16[32,4096]{1,0:T(8,128)(2,1)S(1)}, bf16[32,4096]{1,0:T(8,128)(2,1)S(1)}, u32[]{:S(2)}, u32[]{:S(2)}) collective-permute-start(bf16[32,4096]{1,0:T(8,128)(2,1)S(1)} %get-tuple-element.279), channel_id=1, source_target_pairs={{0,16},{2,18},{4,20},{6,22},{8,24},{10,26},{12,28},{14,30},{16,0},... | collective-permute-start | bytes 786440 | tf_op jit(solution)/shard_map/ppermute | solution.py:991
  134.2 23.5 %collective-permute-start.16 = (bf16[32,4096]{1,0:T(8,128)(2,1)S(1)}, bf16[32,4096]{1,0:T(8,128)(2,1)S(1)}, u32[]{:S(2)}, u32[]{:S(2)}) collective-permute-start(bf16[32,4096]{1,0:T(8,128)(2,1)S(1)} %get-tuple-element.278), channel_id=1, source_target_pairs={{0,24},{2,26},{4,28},{6,30},{8,0},{10,2},{12,4},{14,6},{16,8},{18,... | collective-permute-start | bytes 786440 | tf_op jit(solution)/shard_map/ppermute | solution.py:991
  136.3 16.3 %collective-permute-start.11 = (bf16[128,2048]{1,0:T(8,128)(2,1)S(1)}, bf16[128,2048]{1,0:T(8,128)(2,1)S(1)}, u32[]{:S(2)}, u32[]{:S(2)}) collective-permute-start(bf16[128,2048]{1,0:T(8,128)(2,1)S(1)} %add_convert_fusion.1), channel_id=1, source_target_pairs={{0,4},{2,6},{4,0},{6,2},{8,12},{10,14},{12,8},{14,10},{16,20},{18,... | collective-permute-start | bytes 1572872 | tf_op jit(solution)/shard_map/ppermute | solution.py:1120
  152.6 5.5 %collective-permute-start.13 = (bf16[512,1152]{1,0:T(8,128)(2,1)S(1)}, bf16[512,1152]{1,0:T(8,128)(2,1)S(1)}, u32[]{:S(2)}, u32[]{:S(2)}) collective-permute-start(bf16[512,1152]{1,0:T(8,128)(2,1)S(1)} %get-tuple-element.237), channel_id=1, source_target_pairs={{0,2},{2,0},{4,6},{6,4},{8,10},{10,8},{12,14},{14,12},{16,18},{18,... | collective-permute-start | bytes 3538952 | tf_op jit(solution)/shard_map/ppermute | solution.py:1054
  158.5 9.5 %collective-permute-start.22 = (bf16[128,1152]{1,0:T(8,128)(2,1)S(1)}, bf16[128,1152]{1,0:T(8,128)(2,1)S(1)}, u32[]{:S(2)}, u32[]{:S(2)}) collective-permute-start(bf16[128,1152]{1,0:T(8,128)(2,1)S(1)} %get-tuple-element.276), channel_id=1, source_target_pairs={{0,1},{1,0},{2,3},{3,2},{4,5},{5,4},{6,7},{7,6},{8,9},{9,8},{10,11... | collective-permute-start | bytes 884744 | tf_op jit(solution)/shard_map/ppermute | solution.py:1145
  158.7 11.2 %collective-permute-start.23 = (bf16[128,1152]{1,0:T(8,128)(2,1)S(1)}, bf16[128,1152]{1,0:T(8,128)(2,1)S(1)}, u32[]{:S(2)}, u32[]{:S(2)}) collective-permute-start(bf16[128,1152]{1,0:T(8,128)(2,1)S(1)} %get-tuple-element.275), channel_id=1, source_target_pairs={{0,4},{2,6},{4,0},{6,2},{8,12},{10,14},{12,8},{14,10},{16,20},{18,... | collective-permute-start | bytes 884744 | tf_op jit(solution)/shard_map/ppermute | solution.py:1145
  159.4 15.6 %collective-permute-start.24 = (bf16[128,1152]{1,0:T(8,128)(2,1)S(1)}, bf16[128,1152]{1,0:T(8,128)(2,1)S(1)}, u32[]{:S(2)}, u32[]{:S(2)}) collective-permute-start(bf16[128,1152]{1,0:T(8,128)(2,1)S(1)} %get-tuple-element.274), channel_id=1, source_target_pairs={{0,5},{1,4},{2,7},{3,6},{4,1},{5,0},{6,3},{7,2},{8,13},{9,12},{10,... | collective-permute-start | bytes 884744 | tf_op jit(solution)/shard_map/ppermute | solution.py:1146
  166.7 9.4 %collective-permute-start.18 = (bf16[32,2048]{1,0:T(8,128)(2,1)S(1)}, bf16[32,2048]{1,0:T(8,128)(2,1)S(1)}, u32[]{:S(2)}, u32[]{:S(2)}) collective-permute-start(bf16[32,2048]{1,0:T(8,128)(2,1)S(1)} %get-tuple-element.284), channel_id=1, source_target_pairs={{0,8},{2,10},{4,12},{6,14},{8,16},{10,18},{12,20},{14,22},{16,24},... | collective-permute-start | bytes 393224 | tf_op jit(solution)/shard_map/ppermute | solution.py:991
  166.7 13.2 %collective-permute-start.19 = (bf16[32,2048]{1,0:T(8,128)(2,1)S(1)}, bf16[32,2048]{1,0:T(8,128)(2,1)S(1)}, u32[]{:S(2)}, u32[]{:S(2)}) collective-permute-start(bf16[32,2048]{1,0:T(8,128)(2,1)S(1)} %get-tuple-element.283), channel_id=1, source_target_pairs={{0,16},{2,18},{4,20},{6,22},{8,24},{10,26},{12,28},{14,30},{16,0},... | collective-permute-start | bytes 393224 | tf_op jit(solution)/shard_map/ppermute | solution.py:991
  168.0 14.5 %collective-permute-start.20 = (bf16[32,2048]{1,0:T(8,128)(2,1)S(1)}, bf16[32,2048]{1,0:T(8,128)(2,1)S(1)}, u32[]{:S(2)}, u32[]{:S(2)}) collective-permute-start(bf16[32,2048]{1,0:T(8,128)(2,1)S(1)} %get-tuple-element.282), channel_id=1, source_target_pairs={{0,24},{2,26},{4,28},{6,30},{8,0},{10,2},{12,4},{14,6},{16,8},{18,... | collective-permute-start | bytes 393224 | tf_op jit(solution)/shard_map/ppermute | solution.py:991
  169.9 16.2 %collective-permute-start.17 = (bf16[1024,256]{1,0:T(8,128)(2,1)S(1)}, bf16[1024,256]{1,0:T(8,128)(2,1)S(1)}, u32[]{:S(2)}, u32[]{:S(2)}) collective-permute-start(bf16[1024,256]{1,0:T(8,128)(2,1)S(1)} %get-tuple-element.249), channel_id=1, source_target_pairs={{0,1},{1,0},{2,3},{3,2},{4,5},{5,4},{6,7},{7,6},{8,9},{9,8},{10,11... | collective-permute-start | bytes 1572872 | tf_op jit(solution)/shard_map/ppermute | solution.py:1158
  175.2 13.7 %collective-permute-start.25 = (bf16[32,1152]{1,0:T(8,128)(2,1)S(1)}, bf16[32,1152]{1,0:T(8,128)(2,1)S(1)}, u32[]{:S(2)}, u32[]{:S(2)}) collective-permute-start(bf16[32,1152]{1,0:T(8,128)(2,1)S(1)} %get-tuple-element.288), channel_id=1, source_target_pairs={{0,8},{2,10},{4,12},{6,14},{8,16},{10,18},{12,20},{14,22},{16,24},... | collective-permute-start | bytes 221192 | tf_op jit(solution)/shard_map/ppermute | solution.py:991
  176.1 12.9 %collective-permute-start.26 = (bf16[32,1152]{1,0:T(8,128)(2,1)S(1)}, bf16[32,1152]{1,0:T(8,128)(2,1)S(1)}, u32[]{:S(2)}, u32[]{:S(2)}) collective-permute-start(bf16[32,1152]{1,0:T(8,128)(2,1)S(1)} %get-tuple-element.287), channel_id=1, source_target_pairs={{0,16},{2,18},{4,20},{6,22},{8,24},{10,26},{12,28},{14,30},{16,0},... | collective-permute-start | bytes 221192 | tf_op jit(solution)/shard_map/ppermute | solution.py:991
  179.9 9.1 %collective-permute-start.27 = (bf16[32,1152]{1,0:T(8,128)(2,1)S(1)}, bf16[32,1152]{1,0:T(8,128)(2,1)S(1)}, u32[]{:S(2)}, u32[]{:S(2)}) collective-permute-start(bf16[32,1152]{1,0:T(8,128)(2,1)S(1)} %get-tuple-element.286), channel_id=1, source_target_pairs={{0,24},{2,26},{4,28},{6,30},{8,0},{10,2},{12,4},{14,6},{16,8},{18,... | collective-permute-start | bytes 221192 | tf_op jit(solution)/shard_map/ppermute | solution.py:991
  186.3 6.9 %collective-permute-start.21 = (bf16[32,3072]{1,0:T(8,128)(2,1)S(1)}, bf16[32,3072]{1,0:T(8,128)(2,1)S(1)}, u32[]{:S(2)}, u32[]{:S(2)}) collective-permute-start(bf16[32,3072]{1,0:T(8,128)(2,1)S(1)} %pad_maximum_fusion.2), channel_id=1, source_target_pairs={{0,1},{1,0},{2,3},{3,2},{4,5},{5,4},{6,7},{7,6},{8,9},{9,8},{10,11... | collective-permute-start | bytes 589832 | tf_op jit(solution)/shard_map/ppermute | solution.py:1163
  (78 other events, 832.2 us)
